TPU v7x, 32 devices: a whole 2x2x4 slice. The times are simulated.
32 devices in a mesh: ctx: 8 (over y, x, core), fsdp: 4 (over z).
Axes of the slice: x: 2, y: 2, z: 4, core: 2. Of those that a mesh axis runs over, the one named last changes fastest.
Arguments:
- layer_in: bfloat16 [4, 8, 192, 768], P('fsdp', 'ctx'), may hold values from -6 to 6
- qkv_weight: bfloat16 [768, 2304], P('fsdp'), may hold values from -0.21875 to 0.21875
- query_bias: float32 [768], replicated, may hold values from -3 to 3
- value_bias: float32 [768], replicated, may hold values from -3 to 3
- out_weight: bfloat16 [768, 768], P('fsdp'), may hold values from -1.5 to 1.5
- out_bias: float32 [768], replicated, may hold values from -3 to 3
- fc_weight: bfloat16 [768, 3072], P('fsdp'), may hold values from -0.21875 to 0.21875
- fc_bias: float32 [3072], replicated, may hold values from -3 to 3
- proj_weight: bfloat16 [3072, 768], P('fsdp'), may hold values from -0.109375 to 0.109375
- proj_bias: float32 [768], replicated, may hold values from -3 to 3
- attn_norm_gain: float32 [768], replicated, may hold values from 0.5 to 1.5
- attn_norm_shift: float32 [768], replicated, may hold values from -2 to 2
- mlp_norm_gain: float32 [768], replicated, may hold values from 0.5 to 1.5
- mlp_norm_shift: float32 [768], replicated, may hold values from -2 to 2
- cotangent: bfloat16 [4, 8, 192, 768], P('fsdp', 'ctx'), may hold values from -6 to 6
- pair_table: int32 [8], replicated, may hold values from 0 to 7, each once
Outputs:
- layer_out: bfloat16 [4, 8, 192, 768], P('fsdp', 'ctx')
- grad_in: float32 [4, 8, 192, 768], P('fsdp', 'ctx')
- grad_qkv_weight: float32 [768, 2304], P(('ctx', 'fsdp'))
- grad_query_bias: float32 [768], P(('ctx', 'fsdp'))
- grad_value_bias: float32 [768], P(('ctx', 'fsdp'))
- grad_out_weight: float32 [768, 768], P(('ctx', 'fsdp'))
- grad_out_bias: float32 [768], P(('ctx', 'fsdp'))
- grad_fc_weight: float32 [768, 3072], P(('ctx', 'fsdp'))
- grad_fc_bias: float32 [3072], P(('ctx', 'fsdp'))
- grad_proj_weight: float32 [3072, 768], P(('ctx', 'fsdp'))
- grad_proj_bias: float32 [768], P(('ctx', 'fsdp'))
- grad_attn_norm_gain: float32 [768], P(('ctx', 'fsdp'))
- grad_attn_norm_shift: float32 [768], P(('ctx', 'fsdp'))
- grad_mlp_norm_gain: float32 [768], P(('ctx', 'fsdp'))
- grad_mlp_norm_shift: float32 [768], P(('ctx', 'fsdp'))
Inputs may be any that keep to these rules, and one draw needn't show every extreme that they name: pair_table is a permutation: index c of ctx holds blocks pair_table[c] and 15 - pair_table[c] of every sequence.
All inputs are finite; a program needn't handle non-finite values.
Results may differ from a plain program's by a relative error of at most 0.035.
Values may be sent and summed in bfloat16 or wider, within the bound.
A program may use at most 256 MiB of HBM per device.

v0:
```python
from functools import partial

import jax
import jax.numpy as jnp
from jax import lax
from jax.experimental import pallas as pl
from jax.experimental.pallas import tpu as pltpu
from jax.sharding import PartitionSpec as P

H = 12
HEAD_DIM = 64
BLK = 96


epsilon = 1e-05
masked_score = -1e30


def normalize(values):
    centered = values - jnp.mean(values, axis=-1, keepdims=True)
    inverse = lax.rsqrt(jnp.mean(centered * centered, axis=-1, keepdims=True) + epsilon)
    return (centered * inverse, inverse)


def norm_back(grad_out, normed, inverse, gain):
    scaled = grad_out * gain
    grad_input = inverse * (
        scaled
        - jnp.mean(scaled, axis=-1, keepdims=True)
        - normed * jnp.mean(scaled * normed, axis=-1, keepdims=True)
    )
    return (grad_input, jnp.sum(grad_out * normed, axis=0), jnp.sum(grad_out, axis=0))


def block_positions(pair_table, device, ctx_count):
    pair_index = lax.dynamic_index_in_dim(pair_table, device, 0, keepdims=False)
    column = jnp.arange(2 * BLK, dtype=jnp.int32)
    lower = pair_index * BLK + column
    upper = (2 * ctx_count - 1 - pair_index) * BLK + column - BLK
    return jnp.where(column < BLK, lower, upper)


PAIR = 2 * HEAD_DIM
CHUNK = 8 * 2 * BLK
NT = (((1,), (1,)), ((), ()))


def chunk_of(total):
    return CHUNK if total % CHUNK == 0 else total


def head_only(block, head):
    lane = lax.broadcasted_iota(jnp.int32, block.shape, 1)
    return jnp.where((lane // HEAD_DIM) == head, block, jnp.zeros_like(block))


def head_pick(first, second):
    lane = lax.broadcasted_iota(jnp.int32, first.shape, 1)
    return jnp.where(lane < HEAD_DIM, first, second)


def dot_nt(left, right):
    return lax.dot_general(left, right, NT, preferred_element_type=jnp.float32)


def dot_nn(left, right):
    return jnp.dot(left, right, preferred_element_type=jnp.float32)


def forward_kernel(qpos_ref, kpos_ref, q_ref, k_ref, v_ref, out_ref, lse_ref, max_ref, sum_ref):
    step = pl.program_id(1)
    last = pl.num_programs(1) - 1

    @pl.when(step == 0)
    def _():
        max_ref[...] = jnp.full_like(max_ref, masked_score)
        sum_ref[...] = jnp.zeros_like(sum_ref)
        out_ref[...] = jnp.zeros_like(out_ref)

    allowed = kpos_ref[...] <= qpos_ref[...]
    query, keys, values = q_ref[...], k_ref[...], v_ref[...]
    mixed, factors = [], []
    for head in range(2):
        scores = jnp.where(allowed, dot_nt(head_only(query, head), keys), masked_score)
        old_max = max_ref[head]
        new_max = jnp.maximum(old_max, jnp.max(scores, axis=-1, keepdims=True))
        expd = jnp.exp(scores - new_max)
        factor = jnp.exp(old_max - new_max)
        sum_ref[head] = sum_ref[head] * factor + jnp.sum(expd, axis=-1, keepdims=True)
        max_ref[head] = new_max
        mixed.append(dot_nn(expd.astype(jnp.bfloat16), values))
        factors.append(factor)
    rows = query.shape[0]
    scale = head_pick(*(jnp.broadcast_to(f, (rows, PAIR)) for f in factors))
    out_ref[...] = out_ref[...] * scale + head_pick(mixed[0], mixed[1])

    @pl.when(step == last)
    def _():
        total = head_pick(*(jnp.broadcast_to(sum_ref[h], (rows, PAIR)) for h in range(2)))
        out_ref[...] = out_ref[...] / total
        lse_ref[0] = jnp.concatenate(
            [max_ref[h] + jnp.log(sum_ref[h]) for h in range(2)], axis=-1
        )


def forward_attention(query_pos, key_pos, query, keys_values):
    rows, width = query.shape
    total = keys_values.shape[0]
    chunk = chunk_of(total)
    pairs = width // PAIR
    return pl.pallas_call(
        forward_kernel,
        grid=(pairs, total // chunk),
        in_specs=[
            pl.BlockSpec((rows, 1), lambda h, c: (0, 0)),
            pl.BlockSpec((1, chunk), lambda h, c: (0, c)),
            pl.BlockSpec((rows, PAIR), lambda h, c: (0, h)),
            pl.BlockSpec((chunk, PAIR), lambda h, c: (c, h)),
            pl.BlockSpec((chunk, PAIR), lambda h, c: (c, h + pairs)),
        ],
        out_specs=[
            pl.BlockSpec((rows, PAIR), lambda h, c: (0, h)),
            pl.BlockSpec((1, rows, 2), lambda h, c: (h, 0, 0)),
        ],
        out_shape=[
            jax.ShapeDtypeStruct((rows, width), jnp.float32),
            jax.ShapeDtypeStruct((pairs, rows, 2), jnp.float32),
        ],
        scratch_shapes=[
            pltpu.VMEM((2, rows, 1), jnp.float32),
            pltpu.VMEM((2, rows, 1), jnp.float32),
        ],
        compiler_params=pltpu.CompilerParams(vmem_limit_bytes=40 * 2**20),
        cost_estimate=pl.CostEstimate(
            flops=8 * rows * total * width,
            bytes_accessed=4 * total * width,
            transcendentals=rows * total * H,
        ),
        name="attention_forward",
    )(query_pos[:, None], key_pos[None, :], query, keys_values, keys_values)


def query_kernel(qpos_ref, kpos_ref, q_ref, do_ref, stat_ref, k_ref, v_ref, dq_ref):
    @pl.when(pl.program_id(1) == 0)
    def _():
        dq_ref[...] = jnp.zeros_like(dq_ref)

    allowed = kpos_ref[...] <= qpos_ref[...]
    query, d_out, keys, values = q_ref[...], do_ref[...], k_ref[...], v_ref[...]
    parts = []
    for head in range(2):
        lse = stat_ref[0, :, head : head + 1]
        delta = stat_ref[0, :, head + 2 : head + 3]
        scores = jnp.where(allowed, dot_nt(head_only(query, head), keys), masked_score)
        prob = jnp.exp(scores - lse)
        d_prob = dot_nt(head_only(d_out, head), values)
        d_score = (prob * (d_prob - delta)).astype(jnp.bfloat16)
        parts.append(dot_nn(d_score, keys))
    dq_ref[...] += head_pick(parts[0], parts[1]) * HEAD_DIM ** (-0.5)


def query_gradient(query_pos, key_pos, query, d_out, stats, keys_values):
    rows, width = query.shape
    total = keys_values.shape[0]
    chunk = chunk_of(total)
    pairs = width // PAIR
    return pl.pallas_call(
        query_kernel,
        grid=(pairs, total // chunk),
        in_specs=[
            pl.BlockSpec((rows, 1), lambda h, c: (0, 0)),
            pl.BlockSpec((1, chunk), lambda h, c: (0, c)),
            pl.BlockSpec((rows, PAIR), lambda h, c: (0, h)),
            pl.BlockSpec((rows, PAIR), lambda h, c: (0, h)),
            pl.BlockSpec((1, rows, 4), lambda h, c: (h, 0, 0)),
            pl.BlockSpec((chunk, PAIR), lambda h, c: (c, h)),
            pl.BlockSpec((chunk, PAIR), lambda h, c: (c, h + pairs)),
        ],
        out_specs=pl.BlockSpec((rows, PAIR), lambda h, c: (0, h)),
        out_shape=jax.ShapeDtypeStruct((rows, width), jnp.float32),
        compiler_params=pltpu.CompilerParams(vmem_limit_bytes=40 * 2**20),
        cost_estimate=pl.CostEstimate(
            flops=12 * rows * total * width,
            bytes_accessed=4 * total * width,
            transcendentals=rows * total * H,
        ),
        name="attention_query_gradient",
    )(query_pos[:, None], key_pos[None, :], query, d_out, stats, keys_values, keys_values)


def key_kernel(kpos_ref, qpos_ref, k_ref, v_ref, q_ref, do_ref, stat_ref, dk_ref, dv_ref):
    @pl.when(pl.program_id(1) == 0)
    def _():
        dk_ref[...] = jnp.zeros_like(dk_ref)
        dv_ref[...] = jnp.zeros_like(dv_ref)

    allowed = kpos_ref[...] <= qpos_ref[...]
    keys, values, query, d_out = k_ref[...], v_ref[...], q_ref[...], do_ref[...]
    key_parts, value_parts = [], []
    for head in range(2):
        lse = stat_ref[0, head : head + 1, :]
        delta = stat_ref[0, head + 2 : head + 3, :]
        scores = jnp.where(allowed, dot_nt(head_only(keys, head), query), masked_score)
        prob = jnp.exp(scores - lse)
        value_parts.append(dot_nn(prob.astype(jnp.bfloat16), d_out))
        d_prob = dot_nt(head_only(values, head), d_out)
        d_score = (prob * (d_prob - delta)).astype(jnp.bfloat16)
        key_parts.append(dot_nn(d_score, query))
    dk_ref[...] += head_pick(key_parts[0], key_parts[1])
    dv_ref[...] += head_pick(value_parts[0], value_parts[1])


def key_gradients(key_pos, query_pos, qkv, query_all, d_out_all, stats_all):
    rows = qkv.shape[0]
    total, width = query_all.shape
    chunk = chunk_of(total)
    pairs = width // PAIR
    grad_spec = pl.BlockSpec((rows, PAIR), lambda h, c: (0, h))
    return pl.pallas_call(
        key_kernel,
        grid=(pairs, total // chunk),
        in_specs=[
            pl.BlockSpec((rows, 1), lambda h, c: (0, 0)),
            pl.BlockSpec((1, chunk), lambda h, c: (0, c)),
            pl.BlockSpec((rows, PAIR), lambda h, c: (0, h)),
            pl.BlockSpec((rows, PAIR), lambda h, c: (0, h + pairs)),
            pl.BlockSpec((chunk, PAIR), lambda h, c: (c, h)),
            pl.BlockSpec((chunk, PAIR), lambda h, c: (c, h)),
            pl.BlockSpec((1, 4, chunk), lambda h, c: (h, 0, c)),
        ],
        out_specs=[grad_spec, grad_spec],
        out_shape=[jax.ShapeDtypeStruct((rows, width), jnp.float32)] * 2,
        compiler_params=pltpu.CompilerParams(vmem_limit_bytes=40 * 2**20),
        cost_estimate=pl.CostEstimate(
            flops=16 * rows * total * width,
            bytes_accessed=4 * total * width,
            transcendentals=rows * total * H,
        ),
        name="attention_key_gradients",
    )(key_pos[:, None], query_pos[None, :], qkv, qkv, query_all, d_out_all, stats_all)


def whole_weight(weight):
    share = weight.shape[0] // lax.axis_size("ctx")
    mine = lax.dynamic_slice_in_dim(weight, lax.axis_index("ctx") * share, share, 0)
    return lax.all_gather(mine, ("fsdp", "ctx"), axis=0, tiled=True)


def gather_kernel(chips, shards, count, *refs):
    shares, wholes = refs[:count], refs[count : 2 * count]
    own_sem, z_send, z_recv, c_send, c_recv, k_send, k_recv = refs[2 * count :]
    me, row = lax.axis_index("ctx"), lax.axis_index("fsdp")
    chip, core = me // 2, me % 2
    sibling = (chip * 2 + 1 - core, row)

    def above(step):
        return (me, lax.rem(row + step, shards))

    def across(step):
        return (lax.rem(chip + step, chips) * 2 + core, row)

    barrier = pltpu.get_barrier_semaphore()
    greeted = [above(d) for d in range(1, shards)] + [across(d) for d in range(1, chips)]
    greeted.append(sibling)
    for other in greeted:
        pl.semaphore_signal(barrier, inc=1, device_id=other, device_id_type=pl.DeviceIdType.MESH)
    pl.semaphore_wait(barrier, len(greeted))

    def send(src, dst, send_sem, recv_sem, target):
        copy = pltpu.make_async_remote_copy(
            src_ref=src,
            dst_ref=dst,
            send_sem=send_sem,
            recv_sem=recv_sem,
            device_id=target,
            device_id_type=pl.DeviceIdType.MESH,
        )
        copy.start()
        return copy

    def column(item, index):
        return wholes[item].at[:, index]

    own, along, between, inside = {}, {}, {}, {}
    for i in range(count):
        own[i] = pltpu.make_async_copy(shares[i], wholes[i].at[row, me], own_sem.at[i])
        own[i].start()
        for d in range(1, shards):
            along[i, d] = send(
                shares[i],
                wholes[i].at[row, me],
                z_send.at[i, d - 1],
                z_recv.at[i, d - 1],
                above(d),
            )
    for i in range(count):
        own[i].wait()
        for d in range(1, shards):
            along[i, d].wait_recv()
        for d in range(1, chips):
            mine = column(i, me)
            between[i, d] = send(mine, mine, c_send.at[i, d - 1], c_recv.at[i, d - 1], across(d))
        inside[i, 0] = send(
            column(i, me), column(i, me), k_send.at[i, 0], k_recv.at[i, 0], sibling
        )
    for i in range(count):
        for d in range(1, chips):
            between[i, d].wait_recv()
            came = column(i, lax.rem(chip - d + chips, chips) * 2 + core)
            inside[i, d] = send(came, came, k_send.at[i, d], k_recv.at[i, d], sibling)
    for copy in inside.values():
        copy.wait_recv()
    for copies in (along, between, inside):
        for copy in copies.values():
            copy.wait_send()


def whole_weights(weights):
    ctx_count, shards = lax.axis_size("ctx"), lax.axis_size("fsdp")
    chips = ctx_count // 2
    if ctx_count != 8:
        return [whole_weight(item) for item in weights]
    count = len(weights)
    mine = []
    for item in weights:
        share = item.shape[0] // ctx_count
        mine.append(
            lax.dynamic_slice_in_dim(item, lax.axis_index("ctx") * share, share, 0)
        )
    anywhere = pl.BlockSpec(memory_space=pl.ANY)
    dma = pltpu.SemaphoreType.DMA
    wholes = pl.pallas_call(
        partial(gather_kernel, chips, shards, count),
        in_specs=[anywhere] * count,
        out_specs=[anywhere] * count,
        out_shape=[
            jax.ShapeDtypeStruct((shards, ctx_count) + item.shape, item.dtype) for item in mine
        ],
        scratch_shapes=[
            dma((count,)),
            dma((count, shards - 1)),
            dma((count, shards - 1)),
            dma((count, chips - 1)),
            dma((count, chips - 1)),
            dma((count, chips)),
            dma((count, chips)),
        ],
        compiler_params=pltpu.CompilerParams(collective_id=0, has_side_effects=True),
        name="gather_weights",
    )(*mine)
    return [
        whole.reshape(item.shape[0] * shards, item.shape[1])
        for whole, item in zip(wholes, weights)
    ]


def scatter_kernel(chips, shards, spans, packed, out, own, k_land, c_land, z_land, *sems):
    local, k_send, k_recv, c_send, c_recv, z_send, z_recv = sems
    me, row = lax.axis_index("ctx"), lax.axis_index("fsdp")
    chip, core = me // 2, me % 2
    sibling = (chip * 2 + 1 - core, row)

    def above(step):
        return (me, lax.rem(row + step, shards))

    def across(step):
        return (lax.rem(chip + step, chips) * 2 + core, row)

    barrier = pltpu.get_barrier_semaphore()
    greeted = [above(d) for d in range(1, shards)] + [across(d) for d in range(1, chips)]
    greeted.append(sibling)
    for other in greeted:
        pl.semaphore_signal(barrier, inc=1, device_id=other, device_id_type=pl.DeviceIdType.MESH)
    pl.semaphore_wait(barrier, len(greeted))

    def send(src, dst, send_sem, recv_sem, target):
        copy = pltpu.make_async_remote_copy(
            src_ref=src,
            dst_ref=dst,
            send_sem=send_sem,
            recv_sem=recv_sem,
            device_id=target,
            device_id_type=pl.DeviceIdType.MESH,
        )
        copy.start()
        return copy

    order = list(range(1, chips)) + [0]
    kept, inside, between, along = {}, {}, {}, {}
    for i, span in enumerate(spans):
        rows = pl.ds(*span)
        for d in order:
            part = lax.rem(chip + d, chips)
            inside[i, d] = send(
                packed.at[part, 1 - core, :, rows],
                k_land.at[part, :, rows],
                k_send.at[i, d],
                k_recv.at[i, d],
                sibling,
            )
            kept[i, d] = pltpu.make_async_copy(
                packed.at[part, core, :, rows], own.at[part, :, rows], local.at[i, d]
            )
            kept[i, d].start()
    for i, span in enumerate(spans):
        rows = pl.ds(*span)
        for d in order:
            part = lax.rem(chip + d, chips)
            kept[i, d].wait()
            inside[i, d].wait_recv()

            @pl.loop(0, shards)
            def _(f):
                total = own[part, f, rows].astype(jnp.float32)
                total += k_land[part, f, rows].astype(jnp.float32)
                own[part, f, rows] = total.astype(jnp.bfloat16)

            if d:
                between[i, d] = send(
                    own.at[part, :, rows],
                    c_land.at[d - 1, :, rows],
                    c_send.at[i, d - 1],
                    c_recv.at[i, d - 1],
                    across(d),
                )
    for i, span in enumerate(spans):
        rows = pl.ds(*span)
        for d in range(1, chips):
            between[i, d].wait_recv()

        @pl.loop(0, shards)
        def _(f):
            total = own[chip, f, rows].astype(jnp.float32)
            for d in range(1, chips):
                total += c_land[d - 1, f, rows].astype(jnp.float32)
            own[chip, f, rows] = total.astype(jnp.bfloat16)

        for d in range(1, shards):
            along[i, d] = send(
                own.at[chip, lax.rem(row + d, shards), rows],
                z_land.at[d - 1, rows],
                z_send.at[i, d - 1],
                z_recv.at[i, d - 1],
                above(d),
            )
    for i, span in enumerate(spans):
        rows = pl.ds(*span)
        for d in range(1, shards):
            along[i, d].wait_recv()
        total = own[chip, row, rows].astype(jnp.float32)
        for d in range(1, shards):
            total += z_land[d - 1, rows].astype(jnp.float32)
        out[rows] = total
    for copies in (inside, between, along):
        for copy in copies.values():
            copy.wait_send()


def scatter_packed(packed):
    ctx_count, shards = lax.axis_size("ctx"), lax.axis_size("fsdp")
    _, rows, width = packed.shape
    if ctx_count != 8:
        return scatter(packed.reshape(-1, width)).astype(jnp.float32)
    chips = ctx_count // 2
    first = 16 * (-(-rows // 32))
    spans = ((0, first), (first, rows - first))
    dma = pltpu.SemaphoreType.DMA
    low = jnp.bfloat16
    return pl.pallas_call(
        partial(scatter_kernel, chips, shards, spans),
        in_specs=[pl.BlockSpec(memory_space=pl.ANY)],
        out_specs=pl.BlockSpec(memory_space=pltpu.VMEM),
        out_shape=jax.ShapeDtypeStruct((rows, width), jnp.float32),
        scratch_shapes=[
            pltpu.VMEM((chips, shards, rows, width), low),
            pltpu.VMEM((chips, shards, rows, width), low),
            pltpu.VMEM((chips - 1, shards, rows, width), low),
            pltpu.VMEM((shards - 1, rows, width), low),
            dma((2, chips)),
            dma((2, chips)),
            dma((2, chips)),
            dma((2, chips - 1)),
            dma((2, chips - 1)),
            dma((2, shards - 1)),
            dma((2, shards - 1)),
        ],
        compiler_params=pltpu.CompilerParams(
            collective_id=1, has_side_effects=True, vmem_limit_bytes=44 * 2**20
        ),
        name="sum_gradients",
    )(packed.reshape(chips, 2, shards, rows, width))


def all_positions(pair_table, ctx_count):
    column = jnp.arange(2 * BLK, dtype=jnp.int32)[None, :]
    pair = pair_table[:, None]
    lower = pair * BLK + column
    upper = (2 * ctx_count - 1 - pair) * BLK + column - BLK
    return jnp.where(column < BLK, lower, upper).reshape(-1)


def scatter(term):
    return lax.psum_scatter(term, ("ctx", "fsdp"), scatter_dimension=0, tiled=True)


def per_device(
    layer_in,
    qkv_weight,
    query_bias,
    value_bias,
    out_weight,
    out_bias,
    fc_weight,
    fc_bias,
    proj_weight,
    proj_bias,
    attn_norm_gain,
    attn_norm_shift,
    mlp_norm_gain,
    mlp_norm_shift,
    cotangent,
    pair_table,
):
    ctx_count = lax.axis_size("ctx")
    shards = ctx_count * lax.axis_size("fsdp")
    _, _, rows, width = layer_in.shape
    my_pos = block_positions(pair_table, lax.axis_index("ctx"), ctx_count)
    every_pos = all_positions(pair_table, ctx_count)
    flat_in = layer_in.reshape(rows, width).astype(jnp.float32)
    full_qkv, full_out, full_fc, full_proj = whole_weights(
        (qkv_weight, out_weight, fc_weight, proj_weight)
    )
    normed_one, inverse_one = normalize(flat_in)
    first_in = (normed_one * attn_norm_gain + attn_norm_shift).astype(jnp.bfloat16)
    keys_values = (
        jnp.dot(first_in, full_qkv[:, width:], preferred_element_type=jnp.float32)
        + jnp.concatenate([jnp.zeros_like(value_bias), value_bias])
    ).astype(jnp.bfloat16)
    every_kv = lax.all_gather(keys_values, "ctx", axis=0, tiled=True)
    query = (
        jnp.dot(first_in, full_qkv[:, :width], preferred_element_type=jnp.float32) + query_bias
    ).astype(jnp.bfloat16) * jnp.bfloat16(HEAD_DIM ** (-0.5))
    every_query = lax.all_gather(query, "ctx", axis=0, tiled=True)
    attn_exact, lse = forward_attention(my_pos, every_pos, query, every_kv)
    attended = attn_exact.astype(jnp.bfloat16)
    middle = flat_in + jnp.dot(attended, full_out, preferred_element_type=jnp.float32) + out_bias
    normed_two, inverse_two = normalize(middle)
    second_in = (normed_two * mlp_norm_gain + mlp_norm_shift).astype(jnp.bfloat16)
    pre_act = jnp.dot(second_in, full_fc, preferred_element_type=jnp.float32) + fc_bias
    activated, gelu_back = jax.vjp(partial(jax.nn.gelu, approximate=True), pre_act)
    act_low = activated.astype(jnp.bfloat16)
    result = middle + jnp.dot(act_low, full_proj, preferred_element_type=jnp.float32) + proj_bias
    layer_out = result.astype(jnp.bfloat16).reshape(layer_in.shape)
    d_result = cotangent.reshape(rows, width)
    d_act = jnp.einsum("td,fd->tf", d_result, full_proj, preferred_element_type=jnp.float32)
    (d_pre,) = gelu_back(d_act)
    d_pre_low = d_pre.astype(jnp.bfloat16)
    d_second = jnp.einsum("tf,df->td", d_pre_low, full_fc, preferred_element_type=jnp.float32)
    d_mid_norm, grad_mlp_gain, grad_mlp_shift = norm_back(
        d_second, normed_two, inverse_two, mlp_norm_gain
    )
    d_middle = d_result.astype(jnp.float32) + d_mid_norm
    d_branch = d_middle.astype(jnp.bfloat16)
    d_attended = jnp.einsum(
        "te,de->td", d_branch, full_out, preferred_element_type=jnp.float32
    ).astype(jnp.bfloat16)
    delta = jnp.sum(
        (d_attended.astype(jnp.float32) * attn_exact).reshape(rows, width // PAIR, 2, HEAD_DIM),
        axis=-1,
    )
    stats = jnp.concatenate([lse, jnp.transpose(delta, (1, 0, 2))], axis=-1)
    every_d_out = lax.all_gather(d_attended, "ctx", axis=0, tiled=True)
    every_stat = lax.all_gather(
        jnp.transpose(stats, (0, 2, 1)).reshape(-1, rows), "ctx", axis=1, tiled=True
    ).reshape(width // PAIR, 4, ctx_count * rows)
    grad_proj = jnp.einsum("tf,td->fd", act_low, d_result, preferred_element_type=jnp.float32)
    grad_fc = jnp.einsum("td,tf->df", second_in, d_pre_low, preferred_element_type=jnp.float32)
    grad_out = jnp.einsum("td,te->de", attended, d_branch, preferred_element_type=jnp.float32)
    d_query = query_gradient(my_pos, every_pos, query, d_attended, stats, every_kv)
    d_key, d_value = key_gradients(
        my_pos, every_pos, keys_values, every_query, every_d_out, every_stat
    )
    d_qkv = jnp.concatenate([d_query, d_key, d_value], axis=1).astype(jnp.bfloat16)
    grad_qkv = jnp.einsum("td,te->de", first_in, d_qkv, preferred_element_type=jnp.float32)
    d_first = jnp.einsum("te,de->td", d_qkv, full_qkv, preferred_element_type=jnp.float32)
    d_in_norm, grad_attn_gain, grad_attn_shift = norm_back(
        d_first, normed_one, inverse_one, attn_norm_gain
    )
    grad_in = (d_middle + d_in_norm).reshape(layer_in.shape)
    bias_sum = jnp.sum(d_qkv.astype(jnp.float32), axis=0)
    vectors = (
        bias_sum[:width],
        bias_sum[2 * width :],
        jnp.sum(d_middle, axis=0),
        jnp.sum(d_pre_low.astype(jnp.float32), axis=0),
        jnp.sum(d_result.astype(jnp.float32), axis=0),
        grad_attn_gain,
        grad_attn_shift,
        grad_mlp_gain,
        grad_mlp_shift,
    )
    small = jnp.concatenate([item.reshape(shards, -1) for item in vectors], axis=1)
    lines = 16 * -(-small.shape[1] // (16 * width))
    small = jnp.pad(small, ((0, 0), (0, lines * width - small.shape[1])))
    matrices = (
        [grad_qkv[:, i * width : (i + 1) * width] for i in range(3)]
        + [grad_out]
        + [grad_fc[:, i * width : (i + 1) * width] for i in range(grad_fc.shape[1] // width)]
        + [grad_proj, small.reshape(shards * lines, width)]
    )
    packed = jnp.concatenate(
        [item.astype(jnp.bfloat16).reshape(shards, -1, width) for item in matrices], axis=1
    )
    summed = scatter_packed(packed)
    pieces, start = [], 0
    for item in matrices:
        size = item.shape[0] // shards
        pieces.append(summed[start : start + size])
        start += size
    sum_qkv = jnp.concatenate(pieces[:3], axis=1)
    sum_out = pieces[3]
    sum_fc = jnp.concatenate(pieces[4:-2], axis=1)
    sum_proj = pieces[-2]
    sum_small = pieces[-1].reshape(-1)
    small, start = [], 0
    for item in vectors:
        size = item.shape[0] // shards
        small.append(sum_small[start : start + size])
        start += size
    return (
        layer_out,
        grad_in,
        sum_qkv,
        small[0],
        small[1],
        sum_out,
        small[2],
        sum_fc,
        small[3],
        sum_proj,
        small[4],
        small[5],
        small[6],
        small[7],
        small[8],
    )


def solution(mesh):
    return jax.shard_map(
        per_device,
        mesh=mesh,
        in_specs=(
            P("fsdp", "ctx", None, None),
            P("fsdp", None),
            P(),
            P(),
            P("fsdp", None),
            P(),
            P("fsdp", None),
            P(),
            P("fsdp", None),
            P(),
            P(),
            P(),
            P(),
            P(),
            P("fsdp", "ctx", None, None),
            P(),
        ),
        out_specs=(
            P("fsdp", "ctx", None, None),
            P("fsdp", "ctx", None, None),
            P(("ctx", "fsdp"), None),
            P(("ctx", "fsdp")),
            P(("ctx", "fsdp")),
            P(("ctx", "fsdp"), None),
            P(("ctx", "fsdp")),
            P(("ctx", "fsdp"), None),
            P(("ctx", "fsdp")),
            P(("ctx", "fsdp"), None),
            P(("ctx", "fsdp")),
            P(("ctx", "fsdp")),
            P(("ctx", "fsdp")),
            P(("ctx", "fsdp")),
            P(("ctx", "fsdp")),
        ),
        check_vma=False,
    )
```

profile of v0, /device:TPU:0, one launch (start us, length us, event | category | flops | bytes accessed | tf_op | source)
XLA Modules:
  0.0 382.9 jit_solution(10466890652293326938)
XLA Ops:
  7.2 1.6 constant_dynamic-slice_fusion.3.refs_0_
  15.5 94.8 %gather_weights.1 = (bf16[4,8,24,2304]{3,2,1,0:T(8,128)(2,1)}, bf16[4,8,24,768]{3,2,1,0:T(8,128)(2,1)}, bf16[4,8,24,3072]{3,2,1,0:T(8,128)(2,1)}, bf16[4,8,96,768]{3,2,1,0:T(8,128)(2,1)}) custom-call(bf16[24,2304]{1,0:T(8,128)(2,1)} %constant_dynamic-slice_fusion.3.refs_0_, bf16[24,768]{1,0:T(8,128)(2,1)} %constant_dynamic-slice_fusion.2.refs_1_, ...), custom_call_target="tpu_custom_call" | custom-call | tf_op jit(solution)/shard_map/gather_weights/pallas_call | solution.py:332
  110.4 3.4 fusion.k_ref.v_ref
  113.9 2.4 fusion.15.q_ref
  118.5 41.7 %all-gather.5.cloned.1.call-done.k_ref.v_ref = bf16[1536,1536]{1,0:T(8,128)(2,1)} async-done(((bf16[192,1536]{1,0:T(8,128)(2,1)}), bf16[1536,1536]{1,0:T(8,128)(2,1)}) %all-gather.5.cloned.1.call-update) | async-done | bytes 4718608 | tf_op jit(solution)/shard_map/all_gather | solution.py:539
  160.2 2.3 copy-done.2
  163.5 10.6 %attention_forward.1 = (f32[192,768]{1,0:T(8,128)S(1)}, f32[6,192,2]{2,1,0:T(8,128)S(1)}) custom-call(s32[192,1]{1,0:T(8,128)S(1)} %add_select_fusion.qpos_ref.kpos_ref, s32[1,1536]{1,0:T(1,128)S(1)} %select_n.40.kpos_ref.qpos_ref, bf16[192,768]{1,0:T(8,128)(2,1)S(1)} %copy-done.4, bf16[1536,1536]{1,0:T(8,128)(2,1)S(1)} %copy-done.2, ...), custom_call_target="tpu_custom_call" | custom-call | flops 1811939328 | bytes 4718592 | tf_op jit(solution)/shard_map/attention_forward/pallas_call | solution.py:111
  177.2 3.1 fusion.53
  180.2 2.4 multiply_reduce_fusion
  185.2 2.3 copy.36
  189.0 9.4 %all-gather = f32[8,192,24]{1,2,0:T(8,128)S(1)} all-gather(f32[1,192,24]{1,2,0:T(8,128)S(1)} %bitcast.110), channel_id=1, replica_groups=mesh['ctx'=8,'fsdp'=4] {'ctx'}, dimensions={0}, use_global_device_ids=true | all-gather | bytes 165888 | tf_op jit(solution)/shard_map/all_gather | solution.py:573
  199.0 2.4 copy-done.3
  201.4 8.5 %attention_query_gradient.1 = f32[192,768]{1,0:T(8,128)S(1)} custom-call(s32[192,1]{1,0:T(8,128)S(1)} %add_select_fusion.qpos_ref.kpos_ref, s32[1,1536]{1,0:T(1,128)S(1)} %select_n.40.kpos_ref.qpos_ref, bf16[192,768]{1,0:T(8,128)(2,1)S(1)} %copy-done.5, bf16[192,768]{1,0:T(8,128)(2,1)S(1)} %copy-done.6, f32[6,192,4]{2,1,0:T(8,128)S(1)} %copy.38.stat_ref, ...), custom_call_target="tpu_custom_call" | custom-call | flops 2717908992 | bytes 4718592 | tf_op jit(solution)/shard_map/attention_query_gradient/pallas_call | solution.py:167
  213.7 2.8 convolution_convert_fusion.2
  216.5 2.5 fusion.47
  219.8 4.2 %convolution_convert_fusion.1 = bf16[3072,768]{1,0:T(8,128)(2,1)} fusion(bf16[1,1,192,768]{3,2,1,0:T(8,128)(2,1)S(1)} %copy-done.22, f32[192,3072]{1,0:T(8,128)S(1)} %copy-done.19), kind=kOutput, calls=%fused_computation.1 | convolution fusion | flops 913637376 | bytes 7372800 | tf_op jit(solution)/shard_map/tf,td->fd/dot_general | solution.py:576
  224.1 2.2 fusion.14
  226.3 1.7 copy-done.8
  228.0 1.7 copy-done.9
  229.7 10.5 %attention_key_gradients.1 = (f32[192,768]{1,0:T(8,128)S(1)}, f32[192,768]{1,0:T(8,128)S(1)}) custom-call(s32[192,1]{1,0:T(8,128)S(1)} %add_select_fusion.qpos_ref.kpos_ref, s32[1,1536]{1,0:T(1,128)S(1)} %select_n.40.kpos_ref.qpos_ref, bf16[192,1536]{1,0:T(8,128)(2,1)S(1)} %copy-done.7, bf16[192,1536]{1,0:T(8,128)(2,1)S(1)} %copy-done.7, ...), custom_call_target="tpu_custom_call" | custom-call | flops 3623878656 | bytes 4718592 | tf_op jit(solution)/shard_map/attention_key_gradients/pallas_call | solution.py:219
  240.4 2.7 fusion.32
  254.5 4.7 %constant_dynamic-update-slice_fusion.1 = bf16[4,2,4,304,768]{4,3,2,1,0:T(8,128)(2,1)} fusion(bf16[4,2,4,304,768]{4,3,2,1,0:T(8,128)(2,1)} %constant_dynamic-update-slice_fusion.2, bf16[4,2,4,96,768]{4,3,2,1,0:T(8,128)(2,1)} %bitcast.104), kind=kLoop, calls=%fused_computation.70 | loop fusion | bytes 9437184
  260.2 106.3 %sum_gradients.1 = f32[304,768]{1,0:T(8,128)S(1)} custom-call(bf16[4,2,4,304,768]{4,3,2,1,0:T(8,128)(2,1)} %constant_dynamic-update-slice_fusion.packed), custom_call_target="tpu_custom_call" | custom-call | tf_op jit(solution)/shard_map/sum_gradients/pallas_call | solution.py:469
  372.8 2.1 fusion.31
  (190 shorter events, 40.7 us)
Async XLA Ops:
  7.2 153.0 %all-gather.5.cloned.1.call-start = ((), (), s32[]{:S(2)}) async-start(), calls=%async_computation | async-start | bytes 5308416 | tf_op jit(solution)/shard_map/all_gather | solution.py:539
  12.0 101.8 %copy-start.29 = (f32[192]{0:T(256)}, f32[192]{0:T(256)S(1)}, u32[]{:S(2)}) copy-start(f32[192]{0:T(256)S(1)} %broadcast_multiply_fusion.5) | copy-start | bytes 2308
  13.3 100.6 %copy-start.38 = (f32[192]{0:T(256)}, f32[192]{0:T(256)S(1)}, u32[]{:S(2)}) copy-start(f32[192]{0:T(256)S(1)} %add_rsqrt_fusion.1) | copy-start | bytes 2308
  113.8 112.6 %all-gather.7.cloned.1.call-start = ((), (), s32[]{:S(2)}) async-start(), calls=%async_computation.1 | async-start | bytes 2654208 | tf_op jit(solution)/shard_map/all_gather | solution.py:543
  116.4 110.0 %all-gather.9.cloned.1.call-start = ((), (), s32[]{:S(2)}) async-start(), calls=%async_computation.2 | async-start | bytes 2654208 | tf_op jit(solution)/shard_map/all_gather | solution.py:572
  163.5 10.7 %copy-start.15 = (bf16[4,8,24,768]{3,2,1,0:T(8,128)(2,1)S(1)}, bf16[4,8,24,768]{3,2,1,0:T(8,128)(2,1)}, u32[]{:S(2)}) copy-start(bf16[4,8,24,768]{3,2,1,0:T(8,128)(2,1)} %get-tuple-element.25) | copy-start | bytes 3538948
  163.5 10.7 %copy-start.34 = (f32[768]{0:T(1024)S(1)}, f32[768]{0:T(1024)}, u32[]{:S(2)}) copy-start(f32[768]{0:T(1024)} %param.21) | copy-start | bytes 9220
  163.5 11.4 %copy-start.10 = (bf16[4,8,24,3072]{3,2,1,0:T(8,128)(2,1)S(1)}, bf16[4,8,24,3072]{3,2,1,0:T(8,128)(2,1)}, u32[]{:S(2)}) copy-start(bf16[4,8,24,3072]{3,2,1,0:T(8,128)(2,1)} %get-tuple-element.26) | copy-start | bytes 14155780
  185.1 13.8 %copy-start.5 = (bf16[192,768]{1,0:T(8,128)(2,1)S(1)}, bf16[192,768]{1,0:T(8,128)(2,1)}, u32[]{:S(2)}) copy-start(bf16[192,768]{1,0:T(8,128)(2,1)} %fusion.15.q_ref) | copy-start | bytes 884740
  185.2 13.8 %copy-start.6 = (bf16[192,768]{1,0:T(8,128)(2,1)S(1)}, bf16[192,768]{1,0:T(8,128)(2,1)}, u32[]{:S(2)}) copy-start(bf16[192,768]{1,0:T(8,128)(2,1)} %get-tuple-element.74.do_ref) | copy-start | bytes 884740
  201.4 8.5 %copy-start.32 = (bf16[768]{0:T(1024)(128)(2,1)S(1)}, bf16[768]{0:T(1024)(128)(2,1)}, u32[]{:S(2)}) copy-start(bf16[768]{0:T(1024)(128)(2,1)} %get-tuple-element.39) | copy-start | bytes 4612
  201.4 8.6 %copy-start.33 = (bf16[3072]{0:T(1024)(128)(2,1)S(1)}, bf16[3072]{0:T(1024)(128)(2,1)}, u32[]{:S(2)}) copy-start(bf16[3072]{0:T(1024)(128)(2,1)} %get-tuple-element.76) | copy-start | bytes 18436
  201.4 9.3 %copy-start.42 = (bf16[768]{0:T(1024)(128)(2,1)S(1)}, bf16[768]{0:T(1024)(128)(2,1)}, u32[]{:S(2)}) copy-start(bf16[768]{0:T(1024)(128)(2,1)} %get-tuple-element.31) | copy-start | bytes 4612
  201.4 10.0 %copy-start.41 = (bf16[768]{0:T(1024)(128)(2,1)S(1)}, bf16[768]{0:T(1024)(128)(2,1)}, u32[]{:S(2)}) copy-start(bf16[768]{0:T(1024)(128)(2,1)} %get-tuple-element.37) | copy-start | bytes 4612
  224.1 16.2 %copy-start.30 = (f32[192]{0:T(256)S(1)}, f32[192]{0:T(256)}, u32[]{:S(2)}) copy-start(f32[192]{0:T(256)} %copy-done.29) | copy-start | bytes 2308
  224.1 16.2 %copy-start.36 = (f32[768]{0:T(1024)S(1)}, f32[768]{0:T(1024)}, u32[]{:S(2)}) copy-start(f32[768]{0:T(1024)} %param.26) | copy-start | bytes 9220
  224.1 16.2 %copy-start.39 = (f32[192]{0:T(256)S(1)}, f32[192]{0:T(256)}, u32[]{:S(2)}) copy-start(f32[192]{0:T(256)} %copy-done.38) | copy-start | bytes 2308
  229.7 10.7 %copy-start.47 = (bf16[4,8,24,2304]{3,2,1,0:T(8,128)(2,1)S(1)}, bf16[4,8,24,2304]{3,2,1,0:T(8,128)(2,1)}, u32[]{:S(2)}) copy-start(bf16[4,8,24,2304]{3,2,1,0:T(8,128)(2,1)} %get-tuple-element.23) | copy-start | bytes 10616836
  260.2 112.6 %copy-start.46 = (f32[192]{0:T(256)S(1)}, f32[192]{0:T(256)}, u32[]{:S(2)}) copy-start(f32[192]{0:T(256)} %get-tuple-element.34) | copy-start | bytes 2308
  260.2 112.6 %copy-start.45 = (f32[192]{0:T(256)S(1)}, f32[192]{0:T(256)}, u32[]{:S(2)}) copy-start(f32[192]{0:T(256)} %get-tuple-element.35) | copy-start | bytes 2308
  260.2 112.6 %copy-start.31 = (f32[192]{0:T(256)S(1)}, f32[192]{0:T(256)}, u32[]{:S(2)}) copy-start(f32[192]{0:T(256)} %copy-done.29) | copy-start | bytes 2308
  260.2 112.6 %copy-start.37 = (f32[768]{0:T(1024)S(1)}, f32[768]{0:T(1024)}, u32[]{:S(2)}) copy-start(f32[768]{0:T(1024)} %param.26) | copy-start | bytes 9220
  260.2 112.7 %copy-start.40 = (f32[192]{0:T(256)S(1)}, f32[192]{0:T(256)}, u32[]{:S(2)}) copy-start(f32[192]{0:T(256)} %copy-done.38) | copy-start | bytes 2308
  260.2 116.2 %copy-start.1 = (bf16[192,3072]{1,0:T(8,128)(2,1)S(1)}, bf16[192,3072]{1,0:T(8,128)(2,1)}, u32[]{:S(2)}) copy-start(bf16[192,3072]{1,0:T(8,128)(2,1)} %param.22) | copy-start | bytes 3538948
  (36 other events, 90.2 us)
Sparse Core Ops, SparseCore 0:
  113.9 46.2 all-gather.4
  162.6 29.0 all-gather.6
  194.2 29.0 all-gather.8
where the time goes:
time: 386 us; the launch traced here: 383 us
  Pallas kernels  231 us (60%)
  local copies, waits for them, and re-layouts  47.4 us (12%)
  waiting for transfers between devices  41.7 us (11%)
  matrix products  29.2 us (8%)
  between operations  15.8 us (4%)
  blocking collectives  9.4 us (2%)
  other arithmetic  8.63 us (2%)
    pallas_call x1, Pallas kernels, scatter_packed(): pl.pallas_call(partial(scatter_kernel, chips, shards, spans), in_specs=[p...  106 us
    pallas_call x1, Pallas kernels, whole_weights(): pl.pallas_call(partial(gather_kernel, chips, shards, count), in_specs=[an...  94.8 us
    all_gather x1, waiting for transfers between devices, per_device(): every_kv = lax.all_gather(keys_values, 'ctx', axis=0, tiled=True)  41.7 us
    unnamed x125, local copies, waits for them, and re-layouts  25 us
    pallas_call x1, Pallas kernels, forward_attention(): pl.pallas_call(forward_kernel, grid=(pairs, total // chunk), in_specs=[pl...  10.6 us
    pallas_call x1, Pallas kernels, key_gradients(): pl.pallas_call(key_kernel, grid=(pairs, total // chunk), in_specs=[pl.Blo...  10.5 us
    all_gather x1, blocking collectives, per_device(): lax.all_gather(jnp.transpose(stats, (0, 2, 1)).reshape(-1, rows), 'ctx',...  9.4 us
    pallas_call x1, Pallas kernels, query_gradient(): pl.pallas_call(query_kernel, grid=(pairs, total // chunk), in_specs=[pl.B...  8.48 us
  transfers between devices with their start and end apart: 3, of which 1 were waited for; matrix products, arithmetic and copies ran while one was open for 9% of the time, Pallas kernels for 5%

commit v1 on v0

--- a/solution.py
+++ b/solution.py
@@ -503,6 +503,343 @@
     return lax.psum_scatter(term, ("ctx", "fsdp"), scatter_dimension=0, tiled=True)
 
 
+class Spot:
+    def __init__(self, shards):
+        self.shards = shards
+        self.me, self.row = lax.axis_index("ctx"), lax.axis_index("fsdp")
+        chip, core = self.me // 2, self.me % 2
+        y, x = chip // 2, chip % 2
+        self.core = core
+        self.a = (1 - core) * x + core * y
+        self.b = (1 - core) * y + core * x
+        self.first = self.index(1 - self.a, self.b)
+        self.second = self.index(self.a, 1 - self.b)
+        self.corner = self.index(1 - self.a, 1 - self.b)
+        self.sibling = chip * 2 + 1 - core
+
+    def chip_of(self, a, b):
+        return (1 - self.core) * (2 * b + a) + self.core * (2 * a + b)
+
+    def index(self, a, b):
+        return self.chip_of(a, b) * 2 + self.core
+
+    def near(self, ctx):
+        return (ctx, self.row)
+
+    def above(self, step):
+        return (self.me, lax.rem(self.row + step, self.shards))
+
+    def came(self, step):
+        return lax.rem(self.row - step + self.shards, self.shards)
+
+    def greet(self):
+        barrier = pltpu.get_barrier_semaphore()
+        others = [self.above(d) for d in range(1, self.shards)]
+        others += [self.near(i) for i in (self.first, self.second, self.sibling)]
+        for other in others:
+            pl.semaphore_signal(
+                barrier, inc=1, device_id=other, device_id_type=pl.DeviceIdType.MESH
+            )
+        pl.semaphore_wait(barrier, len(others))
+
+
+def send(src, dst, send_sem, recv_sem, target):
+    copy = pltpu.make_async_remote_copy(
+        src_ref=src,
+        dst_ref=dst,
+        send_sem=send_sem,
+        recv_sem=recv_sem,
+        device_id=target,
+        device_id_type=pl.DeviceIdType.MESH,
+    )
+    copy.start()
+    return copy
+
+
+class Gather:
+    def __init__(self, spot, shard, whole, sems):
+        self.spot, self.shard, self.whole, self.sems = spot, shard, whole, sems
+        self.rows, columns = shard.shape
+        self.half = columns // 2
+        self.copies = {}
+
+    def cols(self):
+        return pl.ds(pl.multiple_of(self.spot.core * self.half, 128), self.half)
+
+    def part(self, row, start, size):
+        begin = pl.multiple_of(row * self.rows + start, 16)
+        return self.whole.at[pl.ds(begin, size), self.cols()]
+
+    def post(self, stage, d, src, dst, target):
+        n = self.spot.shards - 1
+        at = stage * n + d - 1
+        self.copies[stage, d] = send(
+            src, dst, self.sems[0].at[at], self.sems[1].at[at], target
+        )
+
+    def own(self):
+        begin = pl.multiple_of(self.spot.row * self.rows, 16)
+        copy = pltpu.make_async_copy(
+            self.shard, self.whole.at[pl.ds(begin, self.rows)], self.sems[2]
+        )
+        copy.start()
+        return copy
+
+    def along(self):
+        spot, quarter = self.spot, self.rows // 4
+        start = (2 * spot.b + spot.a) * quarter
+        src = self.shard.at[pl.ds(pl.multiple_of(start, 16), quarter), self.cols()]
+        for d in range(1, spot.shards):
+            self.post(0, d, src, self.part(spot.row, start, quarter), spot.above(d))
+
+    def step_one(self):
+        spot, quarter = self.spot, self.rows // 4
+        start = (2 * spot.b + spot.a) * quarter
+        for d in range(1, spot.shards):
+            self.copies[0, d].wait_recv()
+            ref = self.part(spot.came(d), start, quarter)
+            self.post(1, d, ref, ref, spot.near(spot.first))
+
+    def step_two(self):
+        spot, half = self.spot, self.rows // 2
+        for d in range(1, spot.shards):
+            self.copies[1, d].wait_recv()
+            ref = self.part(spot.came(d), spot.b * half, half)
+            self.post(2, d, ref, ref, spot.near(spot.second))
+            self.post(3, d, ref, ref, spot.near(spot.sibling))
+
+    def step_three(self):
+        spot, half = self.spot, self.rows // 2
+        for d in range(1, spot.shards):
+            self.copies[2, d].wait_recv()
+            ref = self.part(spot.came(d), (1 - spot.b) * half, half)
+            self.post(4, d, ref, ref, spot.near(spot.sibling))
+
+    def finish(self):
+        for d in range(1, self.spot.shards):
+            self.copies[3, d].wait_recv()
+            self.copies[4, d].wait_recv()
+
+    def drain(self):
+        for copy in self.copies.values():
+            copy.wait_send()
+
+
+class Exchange:
+    def __init__(self, spot, whole, view, sems):
+        self.spot, self.sems = spot, sems
+        self.view = lambda device: view(whole, device)
+        self.copies = {}
+
+    def post(self, at, device, target):
+        ref = self.view(device)
+        self.copies[at] = send(
+            ref, ref, self.sems[0].at[at], self.sems[1].at[at], self.spot.near(target)
+        )
+
+    def start(self):
+        spot = self.spot
+        self.post(0, spot.me, spot.first)
+        self.post(1, spot.me, spot.second)
+        self.post(2, spot.me, spot.sibling)
+
+    def pass_on(self):
+        spot = self.spot
+        self.copies[0].wait_recv()
+        self.post(3, spot.first, spot.second)
+        self.post(4, spot.first, spot.sibling)
+
+    def share(self):
+        spot = self.spot
+        self.copies[1].wait_recv()
+        self.post(5, spot.second, spot.sibling)
+        self.copies[3].wait_recv()
+        self.post(6, spot.corner, spot.sibling)
+
+    def finish(self):
+        for at in (2, 4, 5, 6):
+            self.copies[at].wait_recv()
+
+    def drain(self):
+        for copy in self.copies.values():
+            copy.wait_send()
+
+
+def front_kernel(
+    shards,
+    x_ref,
+    gain_ref,
+    shift_ref,
+    qbias_ref,
+    vbias_ref,
+    qpos_ref,
+    kpos_ref,
+    qkv_shard,
+    out_shard,
+    fc_shard,
+    proj_shard,
+    first_ref,
+    query_ref,
+    attn_ref,
+    lse_ref,
+    kv_out,
+    qkv_out,
+    out_out,
+    fc_out,
+    proj_out,
+    qkv_ref,
+    kv_ref,
+    *sems,
+):
+    spot = Spot(shards)
+    spot.greet()
+    weights = [
+        Gather(spot, shard, whole, sems[3 * i : 3 * i + 3])
+        for i, (shard, whole) in enumerate(
+            (
+                (qkv_shard, qkv_ref),
+                (out_shard, out_out),
+                (fc_shard, fc_out),
+                (proj_shard, proj_out),
+            )
+        )
+    ]
+    key_sems, value_sems, keep_sem = sems[12:14], sems[14:16], sems[16]
+    qkv, out, fc, proj = weights
+    qkv.along()
+    own = [item.own() for item in weights]
+    normed, _ = normalize(x_ref[...].astype(jnp.float32))
+    first_ref[...] = (normed * gain_ref[...] + shift_ref[...]).astype(jnp.bfloat16)
+    qkv.step_one()
+    out.along()
+    fc.along()
+    qkv.step_two()
+    proj.along()
+    qkv.step_three()
+    own[0].wait()
+    qkv.finish()
+    width = x_ref.shape[1]
+
+    def columns(start):
+        def view(whole, device):
+            return whole.at[device, :, pl.ds(start, width)]
+
+        return view
+
+    first_in = first_ref[...]
+    keys = Exchange(spot, kv_ref, columns(0), key_sems)
+    values = Exchange(spot, kv_ref, columns(width), value_sems)
+    kv_ref[spot.me, :, pl.ds(0, width)] = dot_nn(
+        first_in, qkv_ref[:, pl.ds(width, width)]
+    ).astype(jnp.bfloat16)
+    keys.start()
+    kv_ref[spot.me, :, pl.ds(width, width)] = (
+        dot_nn(first_in, qkv_ref[:, pl.ds(2 * width, width)]) + vbias_ref[...]
+    ).astype(jnp.bfloat16)
+    values.start()
+    query_ref[...] = (
+        (dot_nn(first_in, qkv_ref[:, pl.ds(0, width)]) + qbias_ref[...]).astype(jnp.bfloat16)
+        * jnp.bfloat16(HEAD_DIM ** (-0.5))
+    )
+    keep_qkv = pltpu.make_async_copy(qkv_ref, qkv_out, keep_sem.at[0])
+    keep_qkv.start()
+    keys.pass_on()
+    values.pass_on()
+    out.step_one()
+    fc.step_one()
+    keys.share()
+    values.share()
+    out.step_two()
+    proj.step_one()
+    keys.finish()
+    values.finish()
+    keep_kv = pltpu.make_async_copy(kv_ref, kv_out, keep_sem.at[1])
+    keep_kv.start()
+    allowed = kpos_ref[...] <= qpos_ref[...]
+    rows = x_ref.shape[0]
+    total = kv_ref.shape[0] * rows
+
+    def attend(h):
+        lanes = pl.ds(pl.multiple_of(h * PAIR, PAIR), PAIR)
+        value_lanes = pl.ds(pl.multiple_of(width + h * PAIR, PAIR), PAIR)
+        query = query_ref[:, lanes]
+        keys_all = kv_ref[:, :, lanes].reshape(total, PAIR)
+        values_all = kv_ref[:, :, value_lanes].reshape(total, PAIR)
+        mixed, stats = [], []
+        for head in range(2):
+            scores = jnp.where(allowed, dot_nt(head_only(query, head), keys_all), masked_score)
+            most = jnp.max(scores, axis=-1, keepdims=True)
+            expd = jnp.exp(scores - most)
+            norm = jnp.sum(expd, axis=-1, keepdims=True)
+            mixed.append(dot_nn(expd.astype(jnp.bfloat16), values_all) / norm)
+            stats.append(most + jnp.log(norm))
+        attn_ref[:, lanes] = head_pick(mixed[0], mixed[1])
+        lse_ref[h] = jnp.concatenate(stats, axis=-1)
+
+    pairs = width // PAIR
+    fc.step_two()
+    pl.loop(0, pairs // 2)(attend)
+    out.step_three()
+    proj.step_two()
+    pl.loop(pairs // 2, pairs)(attend)
+    fc.step_three()
+    proj.step_three()
+    for item in (out, fc, proj):
+        item.finish()
+    for copy in own[1:]:
+        copy.wait()
+    for item in (*weights, keys, values):
+        item.drain()
+    keep_qkv.wait()
+    keep_kv.wait()
+
+
+def front(layer_in, gain, shift, qbias, vbias, query_pos, key_pos, weights):
+    shards, ctx_count = lax.axis_size("fsdp"), lax.axis_size("ctx")
+    rows, width = layer_in.shape
+    pairs = width // PAIR
+    low, wide = jnp.bfloat16, jnp.float32
+    dma = pltpu.SemaphoreType.DMA
+    anywhere = pl.BlockSpec(memory_space=pl.ANY)
+    inside = pl.BlockSpec(memory_space=pltpu.VMEM)
+    whole = [jax.ShapeDtypeStruct((w.shape[0] * shards, w.shape[1]), low) for w in weights]
+    kv_shape = (ctx_count, rows, 2 * width)
+    gather_sems = [dma((5 * (shards - 1),)), dma((5 * (shards - 1),)), dma] * 4
+    return pl.pallas_call(
+        partial(front_kernel, shards),
+        in_specs=[inside] * 7 + [anywhere] * 4,
+        out_specs=[inside] * 4 + [anywhere] * 5,
+        out_shape=[
+            jax.ShapeDtypeStruct((rows, width), low),
+            jax.ShapeDtypeStruct((rows, width), low),
+            jax.ShapeDtypeStruct((rows, width), wide),
+            jax.ShapeDtypeStruct((pairs, rows, 2), wide),
+            jax.ShapeDtypeStruct(kv_shape, low),
+        ]
+        + whole,
+        scratch_shapes=[
+            pltpu.VMEM(whole[0].shape, low),
+            pltpu.VMEM(kv_shape, low),
+        ]
+        + gather_sems
+        + [dma((7,))] * 4
+        + [dma((2,))],
+        compiler_params=pltpu.CompilerParams(
+            collective_id=0, has_side_effects=True, vmem_limit_bytes=48 * 2**20
+        ),
+        name="front",
+    )(
+        layer_in,
+        gain[None, :],
+        shift[None, :],
+        qbias[None, :],
+        vbias[None, :],
+        query_pos[:, None],
+        key_pos[None, :],
+        *weights,
+    )
+
+
 def per_device(
     layer_in,
     qkv_weight,
@@ -527,21 +864,46 @@
     my_pos = block_positions(pair_table, lax.axis_index("ctx"), ctx_count)
     every_pos = all_positions(pair_table, ctx_count)
     flat_in = layer_in.reshape(rows, width).astype(jnp.float32)
-    full_qkv, full_out, full_fc, full_proj = whole_weights(
-        (qkv_weight, out_weight, fc_weight, proj_weight)
-    )
     normed_one, inverse_one = normalize(flat_in)
-    first_in = (normed_one * attn_norm_gain + attn_norm_shift).astype(jnp.bfloat16)
-    keys_values = (
-        jnp.dot(first_in, full_qkv[:, width:], preferred_element_type=jnp.float32)
-        + jnp.concatenate([jnp.zeros_like(value_bias), value_bias])
-    ).astype(jnp.bfloat16)
-    every_kv = lax.all_gather(keys_values, "ctx", axis=0, tiled=True)
-    query = (
-        jnp.dot(first_in, full_qkv[:, :width], preferred_element_type=jnp.float32) + query_bias
-    ).astype(jnp.bfloat16) * jnp.bfloat16(HEAD_DIM ** (-0.5))
-    every_query = lax.all_gather(query, "ctx", axis=0, tiled=True)
-    attn_exact, lse = forward_attention(my_pos, every_pos, query, every_kv)
+    if ctx_count == 8:
+        (
+            first_in,
+            query,
+            attn_exact,
+            lse,
+            every_kv,
+            full_qkv,
+            full_out,
+            full_fc,
+            full_proj,
+        ) = front(
+            layer_in.reshape(rows, width),
+            attn_norm_gain,
+            attn_norm_shift,
+            query_bias,
+            value_bias,
+            my_pos,
+            every_pos,
+            (qkv_weight, out_weight, fc_weight, proj_weight),
+        )
+        keys_values = lax.dynamic_index_in_dim(every_kv, lax.axis_index("ctx"), 0, False)
+        every_kv = every_kv.reshape(-1, 2 * width)
+        every_query = lax.all_gather(query, "ctx", axis=0, tiled=True)
+    else:
+        full_qkv, full_out, full_fc, full_proj = whole_weights(
+            (qkv_weight, out_weight, fc_weight, proj_weight)
+        )
+        first_in = (normed_one * attn_norm_gain + attn_norm_shift).astype(jnp.bfloat16)
+        keys_values = (
+            jnp.dot(first_in, full_qkv[:, width:], preferred_element_type=jnp.float32)
+            + jnp.concatenate([jnp.zeros_like(value_bias), value_bias])
+        ).astype(jnp.bfloat16)
+        every_kv = lax.all_gather(keys_values, "ctx", axis=0, tiled=True)
+        query = (
+            jnp.dot(first_in, full_qkv[:, :width], preferred_element_type=jnp.float32) + query_bias
+        ).astype(jnp.bfloat16) * jnp.bfloat16(HEAD_DIM ** (-0.5))
+        every_query = lax.all_gather(query, "ctx", axis=0, tiled=True)
+        attn_exact, lse = forward_attention(my_pos, every_pos, query, every_kv)
     attended = attn_exact.astype(jnp.bfloat16)
     middle = flat_in + jnp.dot(attended, full_out, preferred_element_type=jnp.float32) + out_bias
     normed_two, inverse_two = normalize(middle)

time: 386 us -> 322 us (0.83)
  waiting for transfers between devices: 41.7 us -> 12.4 us
  Pallas kernels: 231 us -> 210 us
  local copies, waits for them, and re-layouts: 47.4 us -> 41.2 us
  matrix products: 29.2 us -> 24.9 us
    all_gather x1 -> x0, waiting for transfers between devices: 41.7 us -> none  [per_device(): every_kv = lax.all_gather(keys_values, 'ctx', axis=0, tiled=True)]
    pallas_call x2 -> x1, Pallas kernels: 105 us -> 84.5 us  [front(): pl.pallas_call(partial(front_kernel, shards), in_specs=[inside] * 7 + [an...]
    all_gather x1, waiting for transfers between devices: 0.01 us -> 12.4 us  [per_device(): every_d_out = lax.all_gather(d_attended, 'ctx', axis=0, tiled=True)]
    dot_general x2 -> x0, matrix products: 5.81 us -> none  [the longest x1 3.36 us: per_device(): jnp.dot(first_in, full_qkv[:, width:], preferred_element_type=jnp.float32)]
    dynamic_slice x4 -> x0, local copies, waits for them, and re-layouts: 5.28 us -> none  [whole_weights(): lax.dynamic_slice_in_dim(item, lax.axis_index('ctx') * share, share, 0)]
    unnamed x125 -> x91, local copies, waits for them, and re-layouts: 25 us -> 25.6 us
  transfers between devices with their start and end apart: 3 -> 2, of which waited for: 1 -> 1; matrix products, arithmetic and copies ran while one was open for 9% -> 9% of each run, Pallas kernels for 5% -> 3%
where the time goes in v1:
time: 322 us; the launch traced here: 319 us
  Pallas kernels  210 us (65%)
  local copies, waits for them, and re-layouts  41.2 us (13%)
  matrix products  24.9 us (8%)
  between operations  16 us (5%)
  waiting for transfers between devices  12.4 us (4%)
  blocking collectives  9.27 us (3%)
  other arithmetic  5.11 us (2%)
    pallas_call x1, Pallas kernels, scatter_packed(): pl.pallas_call(partial(scatter_kernel, chips, shards, spans), in_specs=[p...  106 us
    pallas_call x1, Pallas kernels, front(): pl.pallas_call(partial(front_kernel, shards), in_specs=[inside] * 7 + [an...  84.5 us
    unnamed x91, local copies, waits for them, and re-layouts  25.6 us
    all_gather x1, waiting for transfers between devices, per_device(): every_d_out = lax.all_gather(d_attended, 'ctx', axis=0, tiled=True)  12.4 us
    pallas_call x1, Pallas kernels, key_gradients(): pl.pallas_call(key_kernel, grid=(pairs, total // chunk), in_specs=[pl.Blo...  10.5 us
    all_gather x1, blocking collectives, per_device(): lax.all_gather(jnp.transpose(stats, (0, 2, 1)).reshape(-1, rows), 'ctx',...  9.27 us
    pallas_call x1, Pallas kernels, query_gradient(): pl.pallas_call(query_kernel, grid=(pairs, total // chunk), in_specs=[pl.B...  8.94 us
  transfers between devices with their start and end apart: 2, of which 1 were waited for; matrix products, arithmetic and copies ran while one was open for 9% of the time, Pallas kernels for 3%

profile of v1, /device:TPU:0, one launch (start us, length us, event | category | flops | bytes accessed | tf_op | source)
XLA Modules:
  0.0 319.0 jit_solution(8138141661667183888)
XLA Ops:
  10.7 1.2 dynamic_slice.8
  14.3 1.3 copy-done.4
  17.7 84.5 %front.1 = (bf16[192,768]{1,0:T(8,128)(2,1)S(1)}, bf16[192,768]{1,0:T(8,128)(2,1)}, f32[192,768]{1,0:T(8,128)S(1)}, f32[6,192,2]{2,1,0:T(8,128)S(1)}, bf16[8,192...) custom-call(bf16[192,768]{1,0:T(8,128)(2,1)S(1)} %bitcast.63, ...), custom_call_target="tpu_custom_call" | custom-call | tf_op jit(solution)/shard_map/front/pallas_call | solution.py:808
  103.2 3.7 %convolution_add_fusion = f32[192,3072]{1,0:T(8,128)S(1)} fusion(bf16[768,3072]{1,0:T(8,128)(2,1)} %get-tuple-element.28, f32[3072]{0:T(1024)S(1)} %copy-done.29, f32[192,768]{1,0:T(8,128)S(1)} %get-tuple-element.77, f32[768]{0:T(1024)S(1)} %copy-done.27, f32[768]{0:T(1024)S(1)} %copy-done.26, f32[192]{0:T(256)S(1)} %add_rsqrt_fusion.1, ...), kind=kOutput, calls=%fused_computation.4 | convolution fusion | flops 907296768 | bytes 7687680 | tf_op jit(solution)/shard_map/dot_general | solution.py:911
  107.0 2.6 fusion.39
  109.7 1.9 multiply_reduce_fusion
  111.9 1.5 convert_multiply_fusion
  113.4 1.4 copy.36
  115.2 9.3 %all-gather = f32[8,192,24]{1,2,0:T(8,128)S(1)} all-gather(f32[1,192,24]{1,2,0:T(8,128)S(1)} %bitcast.79), channel_id=1, replica_groups=mesh['ctx'=8,'fsdp'=4] {'ctx'}, dimensions={0}, use_global_device_ids=true | all-gather | bytes 165888 | tf_op jit(solution)/shard_map/all_gather | solution.py:935
  125.0 2.3 copy-done
  127.3 8.9 %attention_query_gradient.1 = f32[192,768]{1,0:T(8,128)S(1)} custom-call(s32[192,1]{1,0:T(8,128)S(1)} %add_select_fusion.qpos_ref.kpos_ref, s32[1,1536]{1,0:T(1,128)S(1)} %select_n.34.kpos_ref.qpos_ref, bf16[192,768]{1,0:T(8,128)(2,1)} %get-tuple-element.30.q_ref, bf16[192,768]{1,0:T(8,128)(2,1)S(1)} %copy-done.3, f32[6,192,4]{2,1,0:T(8,128)S(1)} %copy.38.stat_ref, ...), custom_call_target="tpu_custom_call" | custom-call | flops 2717908992 | bytes 4718592 | tf_op jit(solution)/shard_map/attention_query_gradient/pallas_call | solution.py:167
  139.3 1.5 convolution_convert_fusion.3
  140.8 1.5 convolution_convert_fusion.2
  142.4 2.5 fusion.33
  145.7 4.2 %convolution_convert_fusion.1 = bf16[3072,768]{1,0:T(8,128)(2,1)} fusion(bf16[1,1,192,768]{3,2,1,0:T(8,128)(2,1)S(1)} %copy-done.24, f32[192,3072]{1,0:T(8,128)S(1)} %copy-done.20), kind=kOutput, calls=%fused_computation.1 | convolution fusion | flops 913637376 | bytes 7372800 | tf_op jit(solution)/shard_map/tf,td->fd/dot_general | solution.py:938
  149.9 2.2 fusion.10
  152.1 12.4 %all-gather.6.cloned.1.call-done.do_ref = bf16[1536,768]{1,0:T(8,128)(2,1)} async-done(((bf16[192,768]{1,0:T(8,128)(2,1)}), bf16[1536,768]{1,0:T(8,128)(2,1)}) %all-gather.6.cloned.1.call-update) | async-done | bytes 2359312 | tf_op jit(solution)/shard_map/all_gather | solution.py:934
  164.6 1.7 copy-done.7
  166.2 1.7 copy-done.8
  167.9 10.5 %attention_key_gradients.1 = (f32[192,768]{1,0:T(8,128)S(1)}, f32[192,768]{1,0:T(8,128)S(1)}) custom-call(s32[192,1]{1,0:T(8,128)S(1)} %add_select_fusion.qpos_ref.kpos_ref, s32[1,1536]{1,0:T(1,128)S(1)} %select_n.34.kpos_ref.qpos_ref, bf16[192,1536]{1,0:T(8,128)(2,1)S(1)} %dynamic-slice_bitcast_fusion.k_ref.v_ref, ...), custom_call_target="tpu_custom_call" | custom-call | flops 3623878656 | bytes 4718592 | tf_op jit(solution)/shard_map/attention_key_gradients/pallas_call | solution.py:219
  179.8 1.3 fusion.34
  182.5 4.1 %fusion.21 = (bf16[768]{0:T(1024)(128)(2,1)S(1)}, f32[192]{0:T(256)S(1)}, f32[192]{0:T(256)S(1)}, bf16[768]{0:T(1024)(128)(2,1)S(1)}, f32[192,768]{1,0:T(8,128)}) fusion(f32[192]{0:T(256)S(1)} %copy-done.33, f32[192]{0:T(256)S(1)} %copy-done.31, bf16[1,1,192,768]{3,2,1,0:T(8,128)(2,1)S(1)} %copy-done.2, f32[768]{0:T(1024)S(1)} %copy-done.28, ...), kind=kOutput, calls=%fused_computation.36 | convolution fusion | flops 683604096 | bytes 5317632 | tf_op jit(solution)/shard_map/te,de->td/dot_general | solution.py:947
  195.2 4.8 %constant_dynamic-update-slice_fusion.1 = bf16[4,2,4,304,768]{4,3,2,1,0:T(8,128)(2,1)} fusion(bf16[4,2,4,304,768]{4,3,2,1,0:T(8,128)(2,1)} %constant_dynamic-update-slice_fusion.2, bf16[4,2,4,96,768]{4,3,2,1,0:T(8,128)(2,1)} %bitcast.73), kind=kLoop, calls=%fused_computation.60 | loop fusion | bytes 9437184
  200.9 106.1 %sum_gradients.1 = f32[304,768]{1,0:T(8,128)S(1)} custom-call(bf16[4,2,4,304,768]{4,3,2,1,0:T(8,128)(2,1)} %constant_dynamic-update-slice_fusion.packed), custom_call_target="tpu_custom_call" | custom-call | tf_op jit(solution)/shard_map/sum_gradients/pallas_call | solution.py:469
  (150 shorter events, 29.9 us)
Async XLA Ops:
  7.2 95.2 %copy-start.32 = (f32[768]{0:T(1024)S(1)}, f32[768]{0:T(1024)}, u32[]{:S(2)}) copy-start(f32[768]{0:T(1024)} %param.21) | copy-start | bytes 9220
  7.2 145.0 %all-gather.4.cloned.1.call-start = ((), (), s32[]{:S(2)}) async-start(), calls=%async_computation | async-start | bytes 2654208 | tf_op jit(solution)/shard_map/all_gather | solution.py:891
  17.7 84.6 %copy-start.2 = (bf16[1,1,192,768]{3,2,1,0:T(8,128)(2,1)S(1)}, bf16[1,1,192,768]{3,2,1,0:T(8,128)(2,1)}, u32[]{:S(2)}) copy-start(bf16[1,1,192,768]{3,2,1,0:T(8,128)(2,1)} %param.16) | copy-start | bytes 884740
  102.3 62.2 %all-gather.6.cloned.1.call-start = ((), (), s32[]{:S(2)}) async-start(), calls=%async_computation.1 | async-start | bytes 2654208 | tf_op jit(solution)/shard_map/all_gather | solution.py:934
  102.9 8.7 %copy-start.9 = (f32[192,768]{1,0:T(8,128)}, f32[192,768]{1,0:T(8,128)S(1)}, u32[]{:S(2)}) copy-start(f32[192,768]{1,0:T(8,128)S(1)} %get-tuple-element.77) | copy-start | bytes 1769476
  103.2 3.7 %copy-start.23 = (bf16[1,1,192,768]{3,2,1,0:T(8,128)(2,1)S(1)}, bf16[1,1,192,768]{3,2,1,0:T(8,128)(2,1)}, u32[]{:S(2)}) copy-start(bf16[1,1,192,768]{3,2,1,0:T(8,128)(2,1)} %param.30) | copy-start | bytes 884740
  103.2 3.9 %copy-start.34 = (bf16[3072,768]{1,0:T(8,128)(2,1)S(1)}, bf16[3072,768]{1,0:T(8,128)(2,1)}, u32[]{:S(2)}) copy-start(bf16[3072,768]{1,0:T(8,128)(2,1)} %get-tuple-element.29) | copy-start | bytes 14155780
  103.2 6.4 %slice-start = ((s8[4718592]{0:T(1024)(128)(4,1)}), s8[4194304]{0:T(1024)(128)(4,1)S(1)}, s32[]{:S(2)}) async-start(s8[4718592]{0:T(1024)(128)(4,1)} %bitcast.64), calls=%async_computation.2 | async-start | bytes 8388608
  106.9 2.8 copy-start.19
  107.0 2.6 slice-start.1
  113.4 11.6 %copy-start.3 = (bf16[192,768]{1,0:T(8,128)(2,1)S(1)}, bf16[192,768]{1,0:T(8,128)(2,1)}, u32[]{:S(2)}) copy-start(bf16[192,768]{1,0:T(8,128)(2,1)} %get-tuple-element.80.do_ref) | copy-start | bytes 884740
  125.0 2.3 copy-start
  136.2 3.0 copy-start.12
  136.3 4.5 %copy-start.10 = (f32[192,768]{1,0:T(8,128)S(1)}, f32[192,768]{1,0:T(8,128)}, u32[]{:S(2)}) copy-start(f32[192,768]{1,0:T(8,128)} %copy-done.9) | copy-start | bytes 1769476
  136.9 3.9 %copy-start.22 = (bf16[192,3072]{1,0:T(8,128)(2,1)S(1)}, bf16[192,3072]{1,0:T(8,128)(2,1)}, u32[]{:S(2)}) copy-start(bf16[192,3072]{1,0:T(8,128)(2,1)} %copy-done.21) | copy-start | bytes 3538948
  142.3 3.2 copy-start.20
  142.4 3.4 %copy-start.24 = (bf16[1,1,192,768]{3,2,1,0:T(8,128)(2,1)S(1)}, bf16[1,1,192,768]{3,2,1,0:T(8,128)(2,1)}, u32[]{:S(2)}) copy-start(bf16[1,1,192,768]{3,2,1,0:T(8,128)(2,1)} %param.30) | copy-start | bytes 884740
  142.4 7.5 %slice-start.2 = ((s8[4718592]{0:T(1024)(128)(4,1)}), s8[4194304]{0:T(1024)(128)(4,1)S(1)}, s32[]{:S(2)}) async-start(s8[4718592]{0:T(1024)(128)(4,1)} %bitcast.81), calls=%async_computation.4 | async-start | bytes 8388608
  145.7 4.2 %slice-start.3 = ((s8[4718592]{0:T(1024)(128)(4,1)}), s8[524288]{0:T(1024)(128)(4,1)S(1)}, s32[]{:S(2)}) async-start(s8[4718592]{0:T(1024)(128)(4,1)} %bitcast.81), calls=%async_computation.5 | async-start | bytes 1048576
  145.7 4.2 %copy-start.35 = (f32[768]{0:T(1024)S(1)}, f32[768]{0:T(1024)}, u32[]{:S(2)}) copy-start(f32[768]{0:T(1024)} %param.25) | copy-start | bytes 9220
  189.4 2.3 copy-start.15
  190.6 2.3 copy-start.14
  191.8 2.3 copy-start.13
  307.1 2.6 copy-start.25
  (18 other events, 24.3 us)
Sparse Core Ops, SparseCore 0:
  102.4 30.5 all-gather.3
  135.5 29.0 all-gather.5

commit v2 on v1

--- a/solution.py
+++ b/solution.py
@@ -838,6 +838,423 @@
         key_pos[None, :],
         *weights,
     )
+
+
+class Unit:
+    def __init__(self, spot, packed, lands, sems, store):
+        self.spot, self.packed, self.sems, self.store = spot, packed, sems, store
+        self.core_land, self.first_land, self.second_land, self.z_land = lands
+        self.copies = {}
+
+    def post(self, at, src, dst, target):
+        self.copies[at] = send(src, dst, self.sems[0].at[at], self.sems[1].at[at], target)
+
+    def stage(self, number):
+        (self.cores, self.step_one, self.step_two, self.along, self.finish)[number]()
+
+    def cores(self):
+        spot = self.spot
+        self.post(
+            0, self.packed.at[:, 1 - spot.core], self.core_land, spot.near(spot.sibling)
+        )
+
+    def step_one(self):
+        spot, land, packed = self.spot, self.core_land, self.packed
+        self.copies[0].wait_recv()
+        for k, b in enumerate((1 - spot.b, spot.b)):
+            chip = spot.chip_of(1 - spot.a, b)
+            land[chip] = land[chip] + packed[chip, spot.core]
+            self.post(1 + k, land.at[chip], self.first_land.at[k], spot.near(spot.first))
+        for b in (1 - spot.b, spot.b):
+            chip = spot.chip_of(spot.a, b)
+            land[chip] = land[chip] + packed[chip, spot.core]
+
+    def step_two(self):
+        spot, land = self.spot, self.first_land
+        self.copies[1].wait_recv()
+        land[0] = land[0] + self.core_land[spot.chip_of(spot.a, 1 - spot.b)]
+        self.post(3, land.at[0], self.second_land, spot.near(spot.second))
+        self.copies[2].wait_recv()
+        land[1] = land[1] + self.core_land[spot.chip_of(spot.a, spot.b)]
+
+    def along(self):
+        spot, land = self.spot, self.second_land
+        self.copies[3].wait_recv()
+        land[...] = land[...] + self.first_land[1]
+        for d in range(1, spot.shards):
+            other = lax.rem(spot.row + d, spot.shards)
+            self.post(3 + d, land.at[other], self.z_land.at[d - 1], spot.above(d))
+
+    def finish(self):
+        spot = self.spot
+        total = self.second_land[spot.row].astype(jnp.float32)
+        for d in range(1, spot.shards):
+            self.copies[3 + d].wait_recv()
+            total += self.z_land[d - 1].astype(jnp.float32)
+        self.store(total)
+
+    def drain(self):
+        for at, copy in self.copies.items():
+            if at:
+                copy.wait_send()
+
+
+def dot_tn(left, right):
+    return lax.dot_general(
+        left, right, (((0,), (0,)), ((), ())), preferred_element_type=jnp.float32
+    )
+
+
+PROJ_COLS, FC_COLS, TILE = 256, 1024, 256
+
+
+def back_kernel(
+    shards,
+    x_ref,
+    gain_ref,
+    qpos_ref,
+    kpos_ref,
+    act_ref,
+    d_result_ref,
+    second_ref,
+    d_pre_ref,
+    attended_ref,
+    d_branch_ref,
+    d_middle_ref,
+    first_ref,
+    mlp_ref,
+    stat_col_ref,
+    query_in,
+    d_out_in,
+    stat_in,
+    kv_in,
+    qkv_in,
+    grad_in_ref,
+    g_qkv_ref,
+    g_out_ref,
+    g_fc_ref,
+    g_proj_ref,
+    vec_ref,
+    kv_ref,
+    qkv_ref,
+    qd_ref,
+    stat_ref,
+    d_qkv_ref,
+    vec_land,
+    vec_part,
+    proj_pack,
+    fc_pack,
+    mid_pack,
+    *rest,
+):
+    spot = Spot(shards)
+    rows, width = x_ref.shape
+    pairs = width // PAIR
+    load_sem, qd_send, qd_recv, st_send, st_recv, v_send, v_recv = rest[:7]
+    rest = rest[7:]
+    loads = [
+        pltpu.make_async_copy(src, dst, load_sem.at[i])
+        for i, (src, dst) in enumerate(
+            (
+                (query_in, qd_ref.at[spot.me, :, pl.ds(0, width)]),
+                (d_out_in, qd_ref.at[spot.me, :, pl.ds(width, width)]),
+                (stat_in, stat_ref.at[spot.me]),
+                (kv_in, kv_ref),
+                (qkv_in, qkv_ref),
+            )
+        )
+    ]
+    for copy in loads:
+        copy.start()
+    spot.greet()
+    for copy in loads[:3]:
+        copy.wait()
+    stats = Exchange(spot, stat_ref, lambda whole, device: whole.at[device], (st_send, st_recv))
+    payload = Exchange(spot, qd_ref, lambda whole, device: whole.at[device], (qd_send, qd_recv))
+    payload.start()
+    stats.start()
+
+    units, makers = [], []
+    packs = {"proj": proj_pack, "fc": fc_pack, "mid": mid_pack}
+    used = {"proj": [], "fc": [], "mid": []}
+
+    def make_proj(packed, n):
+        def maker():
+            right = d_result_ref[:, n * PROJ_COLS : (n + 1) * PROJ_COLS]
+
+            @pl.loop(0, 4)
+            def _(chip):
+                share = act_ref.shape[1] // 4
+                left = act_ref[:, pl.ds(pl.multiple_of(chip * share, 128), share)]
+                block = dot_tn(left, right).reshape(packed.shape[1:])
+                packed[chip] = block.astype(jnp.bfloat16)
+
+        return maker
+
+    def make_rows(packed, left_ref, right_ref, start, columns):
+        def maker():
+            left = left_ref[...]
+
+            @pl.loop(0, columns // TILE)
+            def _(n):
+                right = right_ref[:, pl.ds(pl.multiple_of(start + n * TILE, 128), TILE)]
+                block = dot_tn(left, right).reshape(packed.shape[:-1] + (TILE,))
+                packed[..., pl.ds(pl.multiple_of(n * TILE, 128), TILE)] = block.astype(
+                    jnp.bfloat16
+                )
+
+        return maker
+
+    def add(kind, out_ref, n, columns, maker):
+        nonlocal rest
+        slot = len(used[kind]) % 2
+        packed = packs[kind].at[slot]
+
+        def store(total):
+            out_ref[:, n * columns : (n + 1) * columns] = total
+
+        unit = Unit(spot, packed, rest[:4], rest[4:6], store)
+        rest = rest[6:]
+        earlier = used[kind][-2] if len(used[kind]) >= 2 else None
+        used[kind].append(unit)
+        units.append(unit)
+        make = maker(packed)
+
+        def begin():
+            if earlier is not None:
+                earlier.copies[0].wait_send()
+            make()
+
+        makers.append(begin)
+
+    for n in range(3):
+        add("proj", g_proj_ref, n, PROJ_COLS, lambda p, n=n: make_proj(p, n))
+    for n in range(3):
+        add(
+            "fc",
+            g_fc_ref,
+            n,
+            FC_COLS,
+            lambda p, n=n: make_rows(p, second_ref, d_pre_ref, n * FC_COLS, FC_COLS),
+        )
+    add("mid", g_out_ref, 0, width, lambda p: make_rows(p, attended_ref, d_branch_ref, 0, width))
+    for n in range(3):
+        add(
+            "mid",
+            g_qkv_ref,
+            n,
+            width,
+            lambda p, n=n: make_rows(p, first_ref, d_qkv_ref, n * width, width),
+        )
+
+    def slot(number):
+        if number < len(units):
+            makers[number]()
+            units[number].stage(0)
+        for stage in range(4, 0, -1):
+            if 0 <= number - stage < len(units):
+                units[number - stage].stage(stage)
+
+    count = kv_ref.shape[0]
+    total = count * rows
+
+    def query_pair(h):
+        lanes = pl.ds(pl.multiple_of(h * PAIR, PAIR), PAIR)
+        upper = pl.ds(pl.multiple_of(width + h * PAIR, PAIR), PAIR)
+        allowed = kpos_ref[...] <= qpos_ref[...]
+        query, d_out = qd_ref[spot.me, :, lanes], qd_ref[spot.me, :, upper]
+        keys = kv_ref[:, :, lanes].reshape(total, PAIR)
+        values = kv_ref[:, :, upper].reshape(total, PAIR)
+        stat = stat_col_ref[h]
+        parts = []
+        for head in range(2):
+            lse, delta = stat[:, head : head + 1], stat[:, head + 2 : head + 3]
+            scores = jnp.where(allowed, dot_nt(head_only(query, head), keys), masked_score)
+            prob = jnp.exp(scores - lse)
+            d_prob = dot_nt(head_only(d_out, head), values)
+            parts.append(dot_nn((prob * (d_prob - delta)).astype(jnp.bfloat16), keys))
+        d_qkv_ref[:, lanes] = (head_pick(parts[0], parts[1]) * HEAD_DIM ** (-0.5)).astype(
+            jnp.bfloat16
+        )
+
+    def key_pair(h):
+        lanes = pl.ds(pl.multiple_of(h * PAIR, PAIR), PAIR)
+        upper = pl.ds(pl.multiple_of(width + h * PAIR, PAIR), PAIR)
+        last = pl.ds(pl.multiple_of(2 * width + h * PAIR, PAIR), PAIR)
+        keys, values = kv_ref[spot.me, :, lanes], kv_ref[spot.me, :, upper]
+        my_keys = [head_only(keys, head) for head in range(2)]
+        my_values = [head_only(values, head) for head in range(2)]
+        key_parts = [jnp.zeros((rows, PAIR), jnp.float32)] * 2
+        value_parts = [jnp.zeros((rows, PAIR), jnp.float32)] * 2
+        key_pos = qpos_ref[...]
+        for chunk in range(2):
+            part = pl.ds(chunk * count // 2, count // 2)
+            span = total // 2
+            query_pos = kpos_ref[:, chunk * span : (chunk + 1) * span]
+            allowed = key_pos <= query_pos
+            query = qd_ref[part, :, lanes].reshape(span, PAIR)
+            d_out = qd_ref[part, :, upper].reshape(span, PAIR)
+            for head in range(2):
+
+                def line(index):
+                    return jnp.concatenate(
+                        [
+                            stat_ref[chunk * count // 2 + i, pl.ds(index, 1), :]
+                            for i in range(count // 2)
+                        ],
+                        axis=-1,
+                    )
+
+                lse, delta = line(4 * h + head), line(4 * h + 2 + head)
+                scores = jnp.where(allowed, dot_nt(my_keys[head], query), masked_score)
+                prob = jnp.exp(scores - lse)
+                value_parts[head] = value_parts[head] + dot_nn(prob.astype(jnp.bfloat16), d_out)
+                d_prob = dot_nt(my_values[head], d_out)
+                d_score = (prob * (d_prob - delta)).astype(jnp.bfloat16)
+                key_parts[head] = key_parts[head] + dot_nn(d_score, query)
+        d_qkv_ref[:, upper] = head_pick(key_parts[0], key_parts[1]).astype(jnp.bfloat16)
+        d_qkv_ref[:, last] = head_pick(value_parts[0], value_parts[1]).astype(jnp.bfloat16)
+
+    slot(0)
+    payload.pass_on()
+    stats.pass_on()
+    loads[3].wait()
+    slot(1)
+    pl.loop(0, 2)(query_pair)
+    slot(2)
+    pl.loop(2, 4)(query_pair)
+    payload.share()
+    stats.share()
+    slot(3)
+    pl.loop(4, pairs)(query_pair)
+    slot(4)
+    payload.finish()
+    stats.finish()
+    pl.loop(0, 2)(key_pair)
+    slot(5)
+    pl.loop(2, 4)(key_pair)
+    slot(6)
+    pl.loop(4, pairs)(key_pair)
+    slot(7)
+    slot(8)
+    slot(9)
+    loads[4].wait()
+    d_qkv = d_qkv_ref[...]
+    d_first = dot_nt(d_qkv, qkv_ref[...])
+    normed, inverse = normalize(x_ref[...].astype(jnp.float32))
+    d_norm, grad_gain, grad_shift = norm_back(d_first, normed, inverse, gain_ref[...])
+    d_middle = d_middle_ref[...]
+    grad_in_ref[...] = d_middle + d_norm
+
+    def over_tokens(block):
+        return jnp.sum(block.astype(jnp.float32), axis=0, keepdims=True)
+
+    bias_fc = over_tokens(d_pre_ref[...])
+    lines = [
+        over_tokens(d_qkv[:, :width]),
+        over_tokens(d_qkv[:, 2 * width :]),
+        over_tokens(d_middle),
+        over_tokens(d_result_ref[...]),
+        grad_gain[None, :],
+        grad_shift[None, :],
+        mlp_ref[0:1],
+        mlp_ref[1:2],
+    ]
+    lines += [bias_fc[:, i * width : (i + 1) * width] for i in range(bias_fc.shape[1] // width)]
+    vec_part[0] = jnp.zeros_like(vec_part.at[0])
+    for i, item in enumerate(lines):
+        vec_part[0, i : i + 1] = item
+    vec_copies = []
+    for k, other in enumerate((spot.sibling, spot.first, spot.second)):
+        copy = send(
+            vec_part.at[k], vec_land.at[k], v_send.at[k], v_recv.at[k], spot.near(other)
+        )
+        vec_copies.append(copy)
+        slot(10 + k)
+        copy.wait_recv()
+        vec_part[k + 1] = vec_part[k] + vec_land[k]
+    for d in range(1, shards):
+        vec_copies.append(
+            send(
+                vec_part.at[3],
+                vec_land.at[2 + d],
+                v_send.at[2 + d],
+                v_recv.at[2 + d],
+                spot.above(d),
+            )
+        )
+    slot(13)
+    summed = vec_part[3]
+    for d in range(1, shards):
+        vec_copies[2 + d].wait_recv()
+        summed = summed + vec_land[2 + d]
+    vec_ref[...] = summed
+    for copy in vec_copies:
+        copy.wait_send()
+    for kind in used.values():
+        for unit in kind[-2:]:
+            unit.copies[0].wait_send()
+    for unit in units:
+        unit.drain()
+    payload.drain()
+    stats.drain()
+
+
+def back(vmem_args, hbm_args):
+    shards, ctx_count = lax.axis_size("fsdp"), lax.axis_size("ctx")
+    rows, width = vmem_args[0].shape
+    hidden = vmem_args[4].shape[1]
+    low, wide = jnp.bfloat16, jnp.float32
+    dma = pltpu.SemaphoreType.DMA
+    chips = ctx_count // 2
+    devices = ctx_count * shards
+    shapes = (
+        [(hidden // devices, PROJ_COLS)] * (width // PROJ_COLS)
+        + [(width // devices, FC_COLS)] * (hidden // FC_COLS)
+        + [(width // devices, width)] * 4
+    )
+    scratch = [
+        pltpu.VMEM((ctx_count, rows, 2 * width), low),
+        pltpu.VMEM((width, 3 * width), low),
+        pltpu.VMEM((ctx_count, rows, 2 * width), low),
+        pltpu.VMEM((ctx_count,) + hbm_args[2].shape, wide),
+        pltpu.VMEM((rows, 3 * width), low),
+        pltpu.VMEM((2 + shards, 16, width), wide),
+        pltpu.VMEM((4, 16, width), wide),
+    ]
+    for shape in (shapes[0], shapes[width // PROJ_COLS], shapes[-1]):
+        scratch.append(pltpu.VMEM((2, chips, 2, shards) + shape, low))
+    scratch += [dma((5,)), dma((7,)), dma((7,)), dma((7,)), dma((7,))]
+    scratch += [dma((2 + shards,)), dma((2 + shards,))]
+    for shape in shapes:
+        scratch += [
+            pltpu.VMEM((chips, shards) + shape, low),
+            pltpu.VMEM((2, shards) + shape, low),
+            pltpu.VMEM((shards,) + shape, low),
+            pltpu.VMEM((shards - 1,) + shape, low),
+            dma((3 + shards,)),
+            dma((3 + shards,)),
+        ]
+    inside = pl.BlockSpec(memory_space=pltpu.VMEM)
+    anywhere = pl.BlockSpec(memory_space=pl.ANY)
+    return pl.pallas_call(
+        partial(back_kernel, shards),
+        in_specs=[inside] * len(vmem_args) + [anywhere] * len(hbm_args),
+        out_specs=[inside] * 6,
+        out_shape=[
+            jax.ShapeDtypeStruct((rows, width), wide),
+            jax.ShapeDtypeStruct((width // devices, 3 * width), wide),
+            jax.ShapeDtypeStruct((width // devices, width), wide),
+            jax.ShapeDtypeStruct((width // devices, hidden), wide),
+            jax.ShapeDtypeStruct((hidden // devices, width), wide),
+            jax.ShapeDtypeStruct((16, width), wide),
+        ],
+        scratch_shapes=scratch,
+        compiler_params=pltpu.CompilerParams(
+            collective_id=1, has_side_effects=True, vmem_limit_bytes=58 * 2**20
+        ),
+        name="back",
+    )(*vmem_args, *hbm_args)
 
 
 def per_device(
@@ -886,9 +1303,6 @@
             every_pos,
             (qkv_weight, out_weight, fc_weight, proj_weight),
         )
-        keys_values = lax.dynamic_index_in_dim(every_kv, lax.axis_index("ctx"), 0, False)
-        every_kv = every_kv.reshape(-1, 2 * width)
-        every_query = lax.all_gather(query, "ctx", axis=0, tiled=True)
     else:
         full_qkv, full_out, full_fc, full_proj = whole_weights(
             (qkv_weight, out_weight, fc_weight, proj_weight)
@@ -931,6 +1345,54 @@
         axis=-1,
     )
     stats = jnp.concatenate([lse, jnp.transpose(delta, (1, 0, 2))], axis=-1)
+    if ctx_count == 8:
+        grad_in, sum_qkv, sum_out, sum_fc, sum_proj, sums = back(
+            (
+                layer_in.reshape(rows, width),
+                attn_norm_gain[None, :],
+                my_pos[:, None],
+                every_pos[None, :],
+                act_low,
+                d_result,
+                second_in,
+                d_pre_low,
+                attended,
+                d_branch,
+                d_middle,
+                first_in,
+                jnp.stack([grad_mlp_gain, grad_mlp_shift]),
+                stats,
+            ),
+            (
+                query,
+                d_attended,
+                jnp.transpose(stats, (0, 2, 1)).reshape(-1, rows),
+                every_kv,
+                full_qkv,
+            ),
+        )
+        share = width // shards
+        device = lax.axis_index("ctx") * lax.axis_size("fsdp") + lax.axis_index("fsdp")
+        mine = lax.dynamic_slice_in_dim(sums, device * share, share, 1)
+        fc_share = d_pre.shape[1] // shards
+        fc_sum = lax.dynamic_slice_in_dim(sums[8:12].reshape(-1), device * fc_share, fc_share)
+        return (
+            layer_out,
+            grad_in.reshape(layer_in.shape),
+            sum_qkv,
+            mine[0],
+            mine[1],
+            sum_out,
+            mine[2],
+            sum_fc,
+            fc_sum,
+            sum_proj,
+            mine[3],
+            mine[4],
+            mine[5],
+            mine[6],
+            mine[7],
+        )
     every_d_out = lax.all_gather(d_attended, "ctx", axis=0, tiled=True)
     every_stat = lax.all_gather(
         jnp.transpose(stats, (0, 2, 1)).reshape(-1, rows), "ctx", axis=1, tiled=True

time: 322 us -> 232 us (0.72)
  Pallas kernels: 210 us -> 191 us
  local copies, waits for them, and re-layouts: 41.2 us -> 24 us
  matrix products: 24.9 us -> 9.7 us
  between operations: 16 us -> 2.26 us
  waiting for transfers between devices: 12.4 us -> 0 us
  blocking collectives: 9.27 us -> 0 us
    pallas_call x3 -> x1, Pallas kernels: 126 us -> 108 us  [back(): pl.pallas_call(partial(back_kernel, shards), in_specs=[inside] * len(vmem...]
    dot_general x5 -> x0, matrix products: 12.5 us -> none  [the longest x1 4.18 us: per_device(): jnp.einsum('tf,td->fd', act_low, d_result, preferred_element_type=jnp.flo...]
    all_gather x2 -> x0, waiting for transfers between devices: 12.4 us -> none  [the longest x1 12.4 us: per_device(): every_d_out = lax.all_gather(d_attended, 'ctx', axis=0, tiled=True)]
    unnamed x91 -> x55, local copies, waits for them, and re-layouts: 25.6 us -> 14.7 us
    all_gather x1 -> x0, blocking collectives: 9.27 us -> none  [per_device(): lax.all_gather(jnp.transpose(stats, (0, 2, 1)).reshape(-1, rows), 'ctx',...]
    slice x8 -> x1, local copies, waits for them, and re-layouts: 6.45 us -> 0.74 us  [per_device(): sums[8:12].reshape(-1)]
  transfers between devices with their start and end apart: 2 -> 0, of which waited for: 1 -> 0; matrix products, arithmetic and copies ran while one was open for 9% -> 0% of each run, Pallas kernels for 3% -> 0%
where the time goes in v2:
time: 232 us; the launch traced here: 230 us
  Pallas kernels  191 us (82%)
  local copies, waits for them, and re-layouts  24 us (10%)
  matrix products  9.7 us (4%)
  other arithmetic  2.99 us (1%)
    pallas_call x1, Pallas kernels, back(): pl.pallas_call(partial(back_kernel, shards), in_specs=[inside] * len(vmem...  108 us
    pallas_call x1, Pallas kernels, front(): pl.pallas_call(partial(front_kernel, shards), in_specs=[inside] * 7 + [an...  83.8 us
    unnamed x55, local copies, waits for them, and re-layouts  14.7 us

profile of v2, /device:TPU:0, one launch (start us, length us, event | category | flops | bytes accessed | tf_op | source)
XLA Modules:
  0.0 230.4 jit_solution(16389507363129106487)
XLA Ops:
  0.7 1.2 dynamic_slice.10
  6.8 1.0 copy-done
  7.8 1.3 copy-done.2
  9.0 1.2 copy-done.4
  10.2 1.0 copy-done.5
  11.2 83.8 %front.1 = (bf16[192,768]{1,0:T(8,128)(2,1)S(1)}, bf16[192,768]{1,0:T(8,128)(2,1)S(1)}, f32[192,768]{1,0:T(8,128)S(1)}, f32[6,192,2]{2,1,0:T(8,128)S(1)}, bf16[8...) custom-call(bf16[192,768]{1,0:T(8,128)(2,1)S(1)} %bitcast.48, ...), custom_call_target="tpu_custom_call" | custom-call | tf_op jit(solution)/shard_map/front/pallas_call | solution.py:808
  95.0 0.7 copy-done.6
  95.7 0.7 copy-done.7
  97.8 1.4 copy-done.20
  99.1 1.7 multiply_convert_fusion
  100.9 2.5 %fusion.6.d_pre_ref = bf16[192,3072]{1,0:T(8,128)(2,1)S(1)} fusion(f32[192,3072]{1,0:T(8,128)S(1)} %get-tuple-element.66, bf16[3072,768]{1,0:T(8,128)(2,1)S(1)} %bitcast.54, bf16[1,1,192,768]{3,2,1,0:T(8,128)(2,1)S(1)} %copy-done.14), kind=kOutput, calls=%fused_computation.10 | convolution fusion | flops 917766144 | bytes 8552448 | tf_op jit(solution)/shard_map/td,fd->tf/dot_general | solution.py:1331
  103.5 1.8 fusion.10
  105.3 1.9 multiply_reduce_fusion
  107.2 1.1 fusion.13
  108.3 1.3 convert_multiply_fusion
  111.2 1.1 copy.36.stat_col_ref
  112.3 107.6 %back.1 = (f32[192,768]{1,0:T(8,128)}, f32[24,2304]{1,0:T(8,128)}, f32[24,768]{1,0:T(8,128)}, f32[24,3072]{1,0:T(8,128)}, f32[96,768]{1,0:T(8,128)}, /*index=5*/f32[16,768]{1,0:T(8,128)}) custom-call(bf16[192,768]{1,0:T(8,128)(2,1)} %bitcast.47, f32[1,768]{1,0:T(1,128)} %copy-done.9, s32[192,1]{1,0:T(8,128)} %copy-done.3, s32[1,1536]{1,0:T(1,128)} %copy-done.8, ...), custom_call_target="tpu_custom_call" | custom-call | tf_op jit(solution)/shard_map/back/pallas_call | solution.py:1240
  219.9 1.6 dynamic-slice_bitcast_fusion
  221.6 0.7 slice.30
  222.9 1.9 copy.42
  224.8 1.6 copy.43
  226.5 1.5 copy.44
  228.0 1.7 copy.45
  229.7 0.7 copy.46
  (70 shorter events, 7.1 us)
Async XLA Ops:
  4.6 92.2 %copy-start.9 = (f32[1,768]{1,0:T(1,128)}, f32[1,768]{1,0:T(1,128)S(1)}, u32[]{:S(2)}) copy-start(f32[1,768]{1,0:T(1,128)S(1)} %broadcast_in_dim.16.gain_ref) | copy-start | bytes 9220
  6.8 90.0 %copy-start.8 = (s32[1,1536]{1,0:T(1,128)}, s32[1,1536]{1,0:T(1,128)S(1)}, u32[]{:S(2)}) copy-start(s32[1,1536]{1,0:T(1,128)S(1)} %select_n.38.kpos_ref) | copy-start | bytes 18436
  6.8 1.0 copy-start
  7.8 1.3 copy-start.2
  9.0 1.2 copy-start.4
  10.2 1.0 copy-start.5
  11.2 85.6 %copy-start.3 = (s32[192,1]{1,0:T(8,128)}, s32[192,1]{1,0:T(8,128)S(1)}, u32[]{:S(2)}) copy-start(s32[192,1]{1,0:T(8,128)S(1)} %add_select_fusion.qpos_ref) | copy-start | bytes 2308
  11.2 85.6 %copy-start.1 = (bf16[1,1,192,768]{3,2,1,0:T(8,128)(2,1)S(1)}, bf16[1,1,192,768]{3,2,1,0:T(8,128)(2,1)}, u32[]{:S(2)}) copy-start(bf16[1,1,192,768]{3,2,1,0:T(8,128)(2,1)} %param.16) | copy-start | bytes 884740
  11.2 85.6 %copy-start.18 = (f32[768]{0:T(1024)S(1)}, f32[768]{0:T(1024)}, u32[]{:S(2)}) copy-start(f32[768]{0:T(1024)} %param.21) | copy-start | bytes 9220
  95.0 0.7 copy-start.6
  96.4 1.1 copy-start.17
  96.4 1.1 copy-start.19
  96.7 2.5 %copy-start.20 = (bf16[768,3072]{1,0:T(8,128)(2,1)S(1)}, bf16[768,3072]{1,0:T(8,128)(2,1)}, u32[]{:S(2)}) copy-start(bf16[768,3072]{1,0:T(8,128)(2,1)} %get-tuple-element.32) | copy-start | bytes 14155780
  96.7 2.5 %copy-start.21 = (f32[3072]{0:T(1024)S(1)}, f32[3072]{0:T(1024)}, u32[]{:S(2)}) copy-start(f32[3072]{0:T(1024)} %param.23) | copy-start | bytes 36868
  96.8 4.1 %copy-start.11 = (bf16[192,768]{1,0:T(8,128)(2,1)}, bf16[192,768]{1,0:T(8,128)(2,1)S(1)}, u32[]{:S(2)}) copy-start(bf16[192,768]{1,0:T(8,128)(2,1)S(1)} %convert_element_type.31.attended_ref) | copy-start | bytes 884740
  97.6 3.3 %slice-start = ((s8[4718592]{0:T(1024)(128)(4,1)}), s8[4194304]{0:T(1024)(128)(4,1)S(1)}, s32[]{:S(2)}) async-start(s8[4718592]{0:T(1024)(128)(4,1)} %bitcast.53), calls=%async_computation | async-start | bytes 8388608
  99.1 1.7 copy-start.15
  99.1 1.7 copy-start.14
  99.1 1.7 slice-start.1
  100.9 2.6 %copy-start.12 = (bf16[192,3072]{1,0:T(8,128)(2,1)}, bf16[192,3072]{1,0:T(8,128)(2,1)S(1)}, u32[]{:S(2)}) copy-start(bf16[192,3072]{1,0:T(8,128)(2,1)S(1)} %get-tuple-element.65.act_ref) | copy-start | bytes 3538948
  100.9 2.5 %copy-start.22 = (f32[768]{0:T(1024)S(1)}, f32[768]{0:T(1024)}, u32[]{:S(2)}) copy-start(f32[768]{0:T(1024)} %param.25) | copy-start | bytes 9220
  103.4 1.8 copy-start.13
  108.3 2.2 copy-start.10
  219.9 9.7 %copy-start.16 = (f32[96,768]{1,0:T(8,128)S(1)}, f32[96,768]{1,0:T(8,128)}, u32[]{:S(2)}) copy-start(f32[96,768]{1,0:T(8,128)} %get-tuple-element.96) | copy-start | bytes 884740
  (1 other events, 0.7 us)

commit v3 on v0

--- a/solution.py
+++ b/solution.py
@@ -1,4 +1,5 @@
 from functools import partial
+from types import SimpleNamespace
 
 import jax
 import jax.numpy as jnp
@@ -503,6 +504,835 @@
     return lax.psum_scatter(term, ("ctx", "fsdp"), scatter_dimension=0, tiled=True)
 
 
+class Spot:
+    def __init__(self, shards):
+        self.shards = shards
+        self.me, self.row = lax.axis_index("ctx"), lax.axis_index("fsdp")
+        chip, core = self.me // 2, self.me % 2
+        y, x = chip // 2, chip % 2
+        self.core = core
+        self.a = (1 - core) * x + core * y
+        self.b = (1 - core) * y + core * x
+        self.first = self.index(1 - self.a, self.b)
+        self.second = self.index(self.a, 1 - self.b)
+        self.corner = self.index(1 - self.a, 1 - self.b)
+        self.sibling = chip * 2 + 1 - core
+
+    def chip_of(self, a, b):
+        return (1 - self.core) * (2 * b + a) + self.core * (2 * a + b)
+
+    def index(self, a, b):
+        return self.chip_of(a, b) * 2 + self.core
+
+    def near(self, ctx):
+        return (ctx, self.row)
+
+    def above(self, step):
+        return (self.me, lax.rem(self.row + step, self.shards))
+
+    def came(self, step):
+        return lax.rem(self.row - step + self.shards, self.shards)
+
+    def greet(self):
+        barrier = pltpu.get_barrier_semaphore()
+        others = [self.above(d) for d in range(1, self.shards)]
+        others += [self.near(i) for i in (self.first, self.second, self.sibling)]
+        for other in others:
+            pl.semaphore_signal(
+                barrier, inc=1, device_id=other, device_id_type=pl.DeviceIdType.MESH
+            )
+        pl.semaphore_wait(barrier, len(others))
+
+
+def send(src, dst, send_sem, recv_sem, target):
+    copy = pltpu.make_async_remote_copy(
+        src_ref=src,
+        dst_ref=dst,
+        send_sem=send_sem,
+        recv_sem=recv_sem,
+        device_id=target,
+        device_id_type=pl.DeviceIdType.MESH,
+    )
+    copy.start()
+    return copy
+
+
+class Gather:
+    def __init__(self, spot, shard, whole, begin, columns, direct, sems):
+        self.spot, self.shard, self.whole, self.sems = spot, shard, whole, sems
+        self.direct = direct
+        self.rows, self.begin, self.half = shard.shape[0], begin, columns // 2
+        self.copies = {}
+
+    def cols(self):
+        return pl.ds(pl.multiple_of(self.begin + self.spot.core * self.half, 128), self.half)
+
+    def part(self, row, start, size):
+        begin = pl.multiple_of(row * self.rows + start, 16)
+        return self.whole.at[pl.ds(begin, size), self.cols()]
+
+    def post(self, stage, d, src, dst, target):
+        at = stage * (self.spot.shards - 1) + d - 1
+        self.copies[stage, d] = send(
+            src, dst, self.sems[0].at[at], self.sems[1].at[at], target
+        )
+
+    def along(self):
+        spot, quarter = self.spot, self.rows // 4
+        start = (2 * spot.b + spot.a) * quarter
+        if self.direct:
+            quarter, start = self.rows, 0
+        src = self.shard.at[pl.ds(pl.multiple_of(start, 16), quarter), self.cols()]
+        for d in range(1, spot.shards):
+            self.post(0, d, src, self.part(spot.row, start, quarter), spot.above(d))
+
+    def step_one(self):
+        spot, quarter = self.spot, self.rows // 4
+        if self.direct:
+            return
+        start = (2 * spot.b + spot.a) * quarter
+        for d in range(1, spot.shards):
+            self.copies[0, d].wait_recv()
+            ref = self.part(spot.came(d), start, quarter)
+            self.post(1, d, ref, ref, spot.near(spot.first))
+
+    def step_two(self):
+        spot, half = self.spot, self.rows // 2
+        if self.direct:
+            return
+        for d in range(1, spot.shards):
+            self.copies[1, d].wait_recv()
+            ref = self.part(spot.came(d), spot.b * half, half)
+            self.post(2, d, ref, ref, spot.near(spot.second))
+            self.post(3, d, ref, ref, spot.near(spot.sibling))
+
+    def step_three(self, d):
+        spot, half = self.spot, self.rows // 2
+        if self.direct:
+            self.copies[0, d].wait_recv()
+            ref = self.part(spot.came(d), 0, self.rows)
+            self.post(4, d, ref, ref, spot.near(spot.sibling))
+            return
+        self.copies[2, d].wait_recv()
+        ref = self.part(spot.came(d), (1 - spot.b) * half, half)
+        self.post(4, d, ref, ref, spot.near(spot.sibling))
+
+    def finish(self, d):
+        if not self.direct:
+            self.copies[3, d].wait_recv()
+        self.copies[4, d].wait_recv()
+
+    def complete(self):
+        for d in range(1, self.spot.shards):
+            self.step_three(d)
+        for d in range(1, self.spot.shards):
+            self.finish(d)
+
+    def drain(self):
+        for copy in self.copies.values():
+            copy.wait_send()
+
+
+class Exchange:
+    def __init__(self, spot, view, sems):
+        self.spot, self.sems, self.view = spot, sems, view
+        self.copies = {}
+
+    def post(self, at, device, target):
+        ref = self.view(device)
+        self.copies[at] = send(
+            ref, ref, self.sems[0].at[at], self.sems[1].at[at], self.spot.near(target)
+        )
+
+    def start(self):
+        spot = self.spot
+        self.post(0, spot.me, spot.first)
+        self.post(1, spot.me, spot.second)
+        self.post(2, spot.me, spot.sibling)
+
+    def pass_on(self):
+        spot = self.spot
+        self.copies[0].wait_recv()
+        self.post(3, spot.first, spot.second)
+        self.post(4, spot.first, spot.sibling)
+
+    def share(self):
+        spot = self.spot
+        self.copies[1].wait_recv()
+        self.post(5, spot.second, spot.sibling)
+        self.copies[3].wait_recv()
+        self.post(6, spot.corner, spot.sibling)
+
+    def finish(self):
+        for at in (2, 4, 5, 6):
+            self.copies[at].wait_recv()
+
+    def drain(self):
+        for copy in self.copies.values():
+            copy.wait_send()
+
+
+class Unit:
+    def __init__(self, spot, packed, lands, sems, store):
+        self.spot, self.packed, self.sems, self.store = spot, packed, sems, store
+        self.core_land, self.first_land, self.second_land, self.z_land = lands
+        self.copies = {}
+
+    def post(self, at, src, dst, target):
+        self.copies[at] = send(src, dst, self.sems[0].at[at], self.sems[1].at[at], target)
+
+    def cores(self):
+        spot = self.spot
+        self.post(
+            0, self.packed.at[:, 1 - spot.core], self.core_land, spot.near(spot.sibling)
+        )
+
+    def step_one(self):
+        spot, land, packed = self.spot, self.core_land, self.packed
+        self.copies[0].wait_recv()
+        for k, b in enumerate((1 - spot.b, spot.b)):
+            chip = spot.chip_of(1 - spot.a, b)
+            land[chip] = land[chip] + packed[chip, spot.core]
+            self.post(1 + k, land.at[chip], self.first_land.at[k], spot.near(spot.first))
+        for b in (1 - spot.b, spot.b):
+            chip = spot.chip_of(spot.a, b)
+            land[chip] = land[chip] + packed[chip, spot.core]
+
+    def step_two(self):
+        spot, land = self.spot, self.first_land
+        self.copies[1].wait_recv()
+        land[0] = land[0] + self.core_land[spot.chip_of(spot.a, 1 - spot.b)]
+        self.post(3, land.at[0], self.second_land, spot.near(spot.second))
+        self.copies[2].wait_recv()
+        land[1] = land[1] + self.core_land[spot.chip_of(spot.a, spot.b)]
+
+    def along(self):
+        spot, land = self.spot, self.second_land
+        self.copies[3].wait_recv()
+        land[...] = land[...] + self.first_land[1]
+        for d in range(1, spot.shards):
+            other = lax.rem(spot.row + d, spot.shards)
+            self.post(3 + d, land.at[other], self.z_land.at[d - 1], spot.above(d))
+
+    def finish(self):
+        spot = self.spot
+        total = self.second_land[spot.row].astype(jnp.float32)
+        for d in range(1, spot.shards):
+            self.copies[3 + d].wait_recv()
+            total += self.z_land[d - 1].astype(jnp.float32)
+        self.store(total)
+
+    def drain(self):
+        for at, copy in self.copies.items():
+            if at:
+                copy.wait_send()
+
+
+class UnitAlongFirst(Unit):
+    def step_one(self):
+        spot, land, packed = self.spot, self.core_land, self.packed
+        self.copies[0].wait_recv()
+        for chip in range(land.shape[0]):
+            land[chip] = land[chip] + packed[chip, spot.core]
+        for d in range(1, spot.shards):
+            other = lax.rem(spot.row + d, spot.shards)
+            self.post(d, land.at[:, other], self.z_land.at[d - 1], spot.above(d))
+
+    def step_two(self):
+        spot, land, low = self.spot, self.z_land, self.z_land.dtype
+        for d in range(1, spot.shards):
+            self.copies[d].wait_recv()
+
+        def add(chip):
+            total = self.core_land[chip, spot.row].astype(jnp.float32)
+            for d in range(1, spot.shards):
+                total += land[d - 1, chip].astype(jnp.float32)
+            land[0, chip] = total.astype(low)
+
+        for k, b in enumerate((1 - spot.b, spot.b)):
+            chip = spot.chip_of(1 - spot.a, b)
+            add(chip)
+            at = spot.shards + k
+            self.post(at, land.at[0, chip], self.first_land.at[k], spot.near(spot.first))
+        for b in (1 - spot.b, spot.b):
+            add(spot.chip_of(spot.a, b))
+
+    def along(self):
+        spot, land, at = self.spot, self.first_land, self.spot.shards
+        self.copies[at].wait_recv()
+        land[0] = land[0] + self.z_land[0, spot.chip_of(spot.a, 1 - spot.b)]
+        self.post(at + 2, land.at[0], self.second_land, spot.near(spot.second))
+
+    def finish(self):
+        spot, at = self.spot, self.spot.shards
+        total = self.z_land[0, spot.chip_of(spot.a, spot.b)].astype(jnp.float32)
+        self.copies[at + 1].wait_recv()
+        total += self.first_land[1].astype(jnp.float32)
+        self.copies[at + 2].wait_recv()
+        self.store(total + self.second_land[...].astype(jnp.float32))
+
+
+def dot_tn(left, right):
+    return lax.dot_general(
+        left, right, (((0,), (0,)), ((), ())), preferred_element_type=jnp.float32
+    )
+
+
+def gelu_pair(u):
+    inner = 0.7978845608028654
+    cubic = 0.044715
+    square = u * u
+    bend = jnp.tanh(inner * (u + cubic * (u * square)))
+    half = 0.5 * (1.0 + bend)
+    slope = half + 0.5 * u * (1.0 - bend * bend) * (inner * (1.0 + 3.0 * cubic * square))
+    return u * half, slope
+
+
+PROJ_COLS, TILE = 256, 256
+DELAYS = (0, 1, 3, 4, 5)
+DELAYS_ALONG = (0, 1, 5, 6, 7)
+ALONG_FIRST = (0, 1)
+DIRECT = ()
+
+
+def layer_kernel(shards, names, *refs):
+    r = SimpleNamespace(**dict(zip(names, refs)))
+    landings = refs[len(names) :]
+    spot = Spot(shards)
+    rows, width = r.x.shape
+    low = jnp.bfloat16
+    pairs = width // PAIR
+    kv, qd, stat = r.kv, r.qd, r.stat
+    count = kv.shape[0]
+    total = count * rows
+    own = []
+    shards_here = (r.qkv_shard, r.out_shard, r.fc_shard, r.proj_shard)
+    for i, (shard, whole) in enumerate(zip(shards_here, (r.qkv, r.out, r.fc, r.proj))):
+        size = shard.shape[0]
+        begin = pl.multiple_of(spot.row * size, 16)
+        own.append(
+            pltpu.make_async_copy(shard, whole.at[pl.ds(begin, size)], r.own_sem.at[i])
+        )
+        own[-1].start()
+    spot.greet()
+
+    def gather(shard, whole, number, begin, columns):
+        sems = r.gather_send.at[number], r.gather_recv.at[number]
+        return Gather(spot, shard, whole, begin, columns, number in DIRECT, sems)
+
+    hidden = r.fc.shape[1]
+    w_kv = gather(r.qkv_shard, r.qkv, 0, width, 2 * width)
+    w_q = gather(r.qkv_shard, r.qkv, 1, 0, width)
+    w_out = gather(r.out_shard, r.out, 2, 0, width)
+    w_fc = gather(r.fc_shard, r.fc, 3, 0, hidden)
+    w_proj = gather(r.proj_shard, r.proj, 4, 0, width)
+
+    def exchange(number, view):
+        return Exchange(spot, view, (r.ex_send.at[number], r.ex_recv.at[number]))
+
+    def columns_of(ref, start):
+        return lambda device: ref.at[device, :, pl.ds(start, width)]
+
+    x_keys = exchange(0, columns_of(kv, 0))
+    x_values = exchange(1, columns_of(kv, width))
+    x_query = exchange(2, columns_of(qd, 0))
+    x_d_out = exchange(3, columns_of(qd, width))
+    x_stat = exchange(4, lambda device: stat.at[device])
+
+    def vector(ref):
+        return ref[...].reshape(1, -1)
+
+    w_kv.along()
+    w_q.along()
+    table = r.table
+
+    def spread(position, pair):
+        lower = pair * BLK + position
+        upper = (2 * count - 1 - pair) * BLK + position - BLK
+        return jnp.where(position < BLK, lower, upper)
+
+    r.qpos[...] = spread(
+        lax.broadcasted_iota(jnp.int32, (rows, 1), 0), table[spot.me]
+    )
+    lane = lax.broadcasted_iota(jnp.int32, (1, total), 1)
+    key_pos = jnp.zeros((1, total), jnp.int32)
+    for device in range(count):
+        local = lane - device * rows
+        key_pos = jnp.where(
+            (local >= 0) & (local < rows), spread(local, table[device]), key_pos
+        )
+    r.kpos[...] = key_pos
+    normed, _ = normalize(r.x[...].astype(jnp.float32))
+    r.first[...] = (normed * vector(r.attn_gain) + vector(r.attn_shift)).astype(low)
+    first_in = r.first[...]
+    w_kv.step_one()
+    w_out.along()
+    w_fc.along()
+    w_kv.step_two()
+    w_q.step_one()
+    own[0].wait()
+    w_kv.complete()
+    kv[spot.me, :, pl.ds(0, width)] = dot_nn(
+        first_in, r.qkv[:, pl.ds(width, width)]
+    ).astype(low)
+    x_keys.start()
+    kv[spot.me, :, pl.ds(width, width)] = (
+        dot_nn(first_in, r.qkv[:, pl.ds(2 * width, width)]) + vector(r.value_bias)
+    ).astype(low)
+    x_values.start()
+    w_proj.along()
+    w_q.step_two()
+    x_keys.pass_on()
+    w_out.step_one()
+    x_values.pass_on()
+    w_q.complete()
+    qd[spot.me, :, pl.ds(0, width)] = (
+        (dot_nn(first_in, r.qkv[:, pl.ds(0, width)]) + vector(r.query_bias)).astype(low)
+        * jnp.bfloat16(HEAD_DIM ** (-0.5))
+    )
+    w_out.step_two()
+    w_fc.step_one()
+    x_keys.share()
+    x_values.share()
+    w_proj.step_one()
+    w_fc.step_two()
+    x_keys.finish()
+    x_values.finish()
+
+    stat_lane = lax.broadcasted_iota(jnp.int32, r.stat_mine.shape, 1)
+
+    def put_stat(index, column):
+        r.stat_mine[...] = jnp.where(stat_lane == index, column, r.stat_mine[...])
+
+    def take_stat(index):
+        return jnp.sum(
+            jnp.where(stat_lane == index, r.stat_mine[...], 0.0), axis=-1, keepdims=True
+        )
+
+    r.stat_mine[...] = jnp.zeros_like(r.stat_mine)
+
+    def lanes_of(h, start=0):
+        return pl.ds(pl.multiple_of(start + h * PAIR, PAIR), PAIR)
+
+    def attend(h):
+        allowed = r.kpos[...] <= r.qpos[...]
+        query = qd[spot.me, :, lanes_of(h)]
+        keys = kv[:, :, lanes_of(h)].reshape(total, PAIR)
+        values = kv[:, :, lanes_of(h, width)].reshape(total, PAIR)
+        mixed = []
+        for head in range(2):
+            scores = jnp.where(allowed, dot_nt(head_only(query, head), keys), masked_score)
+            most = jnp.max(scores, axis=-1, keepdims=True)
+            expd = jnp.exp(scores - most)
+            norm = jnp.sum(expd, axis=-1, keepdims=True)
+            mixed.append(dot_nn(expd.astype(low), values) / norm)
+            put_stat(4 * h + head, most + jnp.log(norm))
+        r.attn[:, lanes_of(h)] = head_pick(mixed[0], mixed[1])
+
+    pl.loop(0, 2)(attend)
+    w_out.complete()
+    w_proj.step_two()
+    pl.loop(2, 4)(attend)
+    x_query.start()
+    pl.loop(4, pairs)(attend)
+    own[1].wait()
+    attended = r.attn[...].astype(low)
+    middle = r.x[...].astype(jnp.float32) + dot_nn(attended, r.out[...]) + vector(r.out_bias)
+    r.middle[...] = middle
+    normed, _ = normalize(middle)
+    r.second[...] = (normed * vector(r.mlp_gain) + vector(r.mlp_shift)).astype(low)
+    r.fc_line[...] = vector(r.fc_bias)
+    own[2].wait()
+    w_fc.complete()
+    own[3].wait()
+    piece = hidden // shards
+    for d in range(shards):
+        if d:
+            w_proj.finish(d)
+        n = spot.came(d)
+        lanes = pl.ds(pl.multiple_of(n * piece, 128), piece)
+        share = pl.ds(pl.multiple_of(n * piece, 16), piece)
+        pre = dot_nn(r.second[...], r.fc[:, lanes]) + r.fc_line[:, lanes]
+        activated, slope = gelu_pair(pre)
+        activated = activated.astype(low)
+        r.act[:, lanes] = activated
+        result = dot_nn(activated, r.proj[share])
+        d_act = dot_nt(r.cot[...], r.proj[share])
+        d_pre = (d_act * slope).astype(low)
+        r.d_pre[:, lanes] = d_pre
+        d_second = dot_nt(d_pre, r.fc[:, lanes])
+        if d:
+            r.result[...] += result
+            r.d_second[...] += d_second
+        else:
+            r.result[...] = result
+            r.d_second[...] = d_second
+            for k in range(1, shards):
+                w_proj.step_three(k)
+            x_query.pass_on()
+
+    units, makers = [], []
+    used = ([], [])
+
+    def make_proj(packed, n):
+        right = r.cot[:, n * PROJ_COLS : (n + 1) * PROJ_COLS]
+
+        @pl.loop(0, 4)
+        def _(chip):
+            share = hidden // 4
+            left = r.act[:, pl.ds(pl.multiple_of(chip * share, 128), share)]
+            packed[chip] = dot_tn(left, right).reshape(packed.shape[1:]).astype(low)
+
+    def make_rows(packed, left_ref, right_ref, start):
+        left = left_ref[...]
+
+        @pl.loop(0, width // TILE)
+        def _(n):
+            right = right_ref[:, pl.ds(pl.multiple_of(start + n * TILE, 128), TILE)]
+            block = dot_tn(left, right).reshape(packed.shape[:-1] + (TILE,))
+            packed[..., pl.ds(pl.multiple_of(n * TILE, 128), TILE)] = block.astype(low)
+
+    def add(kind, out_ref, start, columns, make):
+        packs = (r.mid_pack, r.proj_pack)[kind]
+        slots = packs.shape[0]
+        packed = packs.at[len(used[kind]) % slots]
+        number = len(units)
+
+        def store(total):
+            out_ref[:, start : start + columns] = total
+
+        lands = landings[4 * number : 4 * number + 4]
+        sems = r.unit_send.at[number], r.unit_recv.at[number]
+        kind_of = UnitAlongFirst if number in ALONG_FIRST else Unit
+        unit = kind_of(spot, packed, lands, sems, store)
+        earlier = used[kind][-slots] if len(used[kind]) >= slots else None
+        used[kind].append(unit)
+        units.append(unit)
+
+        def begin():
+            if earlier is not None:
+                earlier.copies[0].wait_send()
+            make(packed)
+            unit.cores()
+
+        makers.append(begin)
+
+    for n in range(hidden // width):
+        add(0, r.g_fc, n * width, width, lambda p, n=n: make_rows(p, r.second, r.d_pre, n * width))
+    for n in range(width // PROJ_COLS):
+        add(1, r.g_proj, n * PROJ_COLS, PROJ_COLS, lambda p, n=n: make_proj(p, n))
+    add(0, r.g_out, 0, width, lambda p: make_rows(p, r.attended, r.d_branch, 0))
+    for n in range(3):
+        add(0, r.g_qkv, n * width, width, lambda p, n=n: make_rows(p, r.first, r.d_qkv, n * width))
+
+    def slot(number):
+        if number < len(units):
+            makers[number]()
+        for stage in range(1, 5):
+            for i, unit in enumerate(units):
+                delays = DELAYS_ALONG if i in ALONG_FIRST else DELAYS
+                if number - i == delays[stage]:
+                    (unit.step_one, unit.step_two, unit.along, unit.finish)[stage - 1]()
+
+    slot(0)
+    middle = r.middle[...]
+    r.layer_out[...] = (middle + r.result[...] + vector(r.proj_bias)).astype(low)
+    normed, inverse = normalize(middle)
+    d_norm, grad_mlp_gain, grad_mlp_shift = norm_back(
+        r.d_second[...], normed, inverse, vector(r.mlp_gain)
+    )
+    d_middle = r.cot[...].astype(jnp.float32) + d_norm
+    r.d_middle[...] = d_middle
+    d_branch = d_middle.astype(low)
+    r.d_branch[...] = d_branch
+    d_attended = dot_nt(d_branch, r.out[...]).astype(low)
+    qd[spot.me, :, pl.ds(width, width)] = d_attended
+    x_d_out.start()
+    r.attended[...] = r.attn[...].astype(low)
+
+    def deltas(h):
+        d_out = qd[spot.me, :, lanes_of(h, width)].astype(jnp.float32)
+        both = d_out * r.attn[:, lanes_of(h)]
+        for head in range(2):
+            put_stat(4 * h + 2 + head, jnp.sum(head_only(both, head), axis=-1, keepdims=True))
+
+    pl.loop(0, pairs)(deltas)
+    stat[spot.me] = jnp.transpose(r.stat_mine[...])[: stat.shape[1]]
+    x_stat.start()
+    x_query.share()
+    slot(1)
+    x_d_out.pass_on()
+    x_stat.pass_on()
+
+    def query_pair(h):
+        allowed = r.kpos[...] <= r.qpos[...]
+        query, d_out = qd[spot.me, :, lanes_of(h)], qd[spot.me, :, lanes_of(h, width)]
+        keys = kv[:, :, lanes_of(h)].reshape(total, PAIR)
+        values = kv[:, :, lanes_of(h, width)].reshape(total, PAIR)
+        parts = []
+        for head in range(2):
+            lse, delta = take_stat(4 * h + head), take_stat(4 * h + 2 + head)
+            scores = jnp.where(allowed, dot_nt(head_only(query, head), keys), masked_score)
+            prob = jnp.exp(scores - lse)
+            d_prob = dot_nt(head_only(d_out, head), values)
+            parts.append(dot_nn((prob * (d_prob - delta)).astype(low), keys))
+        d_query = head_pick(parts[0], parts[1]) * HEAD_DIM ** (-0.5)
+        r.d_qkv[:, lanes_of(h)] = d_query.astype(low)
+
+    def key_pair(h):
+        keys, values = kv[spot.me, :, lanes_of(h)], kv[spot.me, :, lanes_of(h, width)]
+        my_keys = [head_only(keys, head) for head in range(2)]
+        my_values = [head_only(values, head) for head in range(2)]
+        key_parts = [jnp.zeros((rows, PAIR), jnp.float32)] * 2
+        value_parts = [jnp.zeros((rows, PAIR), jnp.float32)] * 2
+        half = count // 2
+        span = half * rows
+        for chunk in range(2):
+            part = pl.ds(chunk * half, half)
+            allowed = r.qpos[...] <= r.kpos[:, chunk * span : (chunk + 1) * span]
+            query = qd[part, :, lanes_of(h)].reshape(span, PAIR)
+            d_out = qd[part, :, lanes_of(h, width)].reshape(span, PAIR)
+
+            def line(index):
+                parts = [stat[chunk * half + i, pl.ds(index, 1), :] for i in range(half)]
+                return jnp.concatenate(parts, axis=-1)
+
+            for head in range(2):
+                lse, delta = line(4 * h + head), line(4 * h + 2 + head)
+                scores = jnp.where(allowed, dot_nt(my_keys[head], query), masked_score)
+                prob = jnp.exp(scores - lse)
+                value_parts[head] = value_parts[head] + dot_nn(prob.astype(low), d_out)
+                d_prob = dot_nt(my_values[head], d_out)
+                d_score = (prob * (d_prob - delta)).astype(low)
+                key_parts[head] = key_parts[head] + dot_nn(d_score, query)
+        r.d_qkv[:, lanes_of(h, width)] = head_pick(*key_parts).astype(low)
+        r.d_qkv[:, lanes_of(h, 2 * width)] = head_pick(*value_parts).astype(low)
+
+    slot(2)
+    pl.loop(0, 2)(query_pair)
+    x_d_out.share()
+    x_stat.share()
+    slot(3)
+    pl.loop(2, 4)(query_pair)
+    slot(4)
+    pl.loop(4, pairs)(query_pair)
+    x_query.finish()
+    x_d_out.finish()
+    x_stat.finish()
+    slot(5)
+    pl.loop(0, 2)(key_pair)
+    slot(6)
+    pl.loop(2, 4)(key_pair)
+    slot(7)
+    pl.loop(4, pairs)(key_pair)
+    for number in range(8, 11):
+        slot(number)
+    d_qkv = r.d_qkv[...]
+    d_first = dot_nt(d_qkv, r.qkv[...])
+    normed, inverse = normalize(r.x[...].astype(jnp.float32))
+    d_norm, grad_gain, grad_shift = norm_back(d_first, normed, inverse, vector(r.attn_gain))
+    d_middle = r.d_middle[...]
+    r.grad_in[...] = d_middle + d_norm
+
+    def over_tokens(block):
+        return jnp.sum(block.astype(jnp.float32), axis=0, keepdims=True)
+
+    bias_fc = over_tokens(r.d_pre[...])
+    lines = [
+        over_tokens(d_qkv[:, :width]),
+        over_tokens(d_qkv[:, 2 * width :]),
+        over_tokens(d_middle),
+        over_tokens(r.cot[...]),
+        grad_gain.reshape(1, -1),
+        grad_shift.reshape(1, -1),
+        grad_mlp_gain.reshape(1, -1),
+        grad_mlp_shift.reshape(1, -1),
+    ]
+    lines += [bias_fc[:, i * width : (i + 1) * width] for i in range(hidden // width)]
+    vec_land, vec_part = r.vec_land, r.vec_part
+    vec_part[0] = jnp.zeros(vec_part.shape[1:], jnp.float32)
+    for i, item in enumerate(lines):
+        vec_part[0, i : i + 1] = item
+    vec_copies = []
+
+    def vec_post(k, src, target):
+        copy = send(src, vec_land.at[k], r.vec_send.at[k], r.vec_recv.at[k], target)
+        vec_copies.append(copy)
+        return copy
+
+    for k, other in enumerate((spot.sibling, spot.first, spot.second)):
+        copy = vec_post(k, vec_part.at[k], spot.near(other))
+        slot(len(units) + k)
+        copy.wait_recv()
+        vec_part[k + 1] = vec_part[k] + vec_land[k]
+    for d in range(1, shards):
+        vec_post(2 + d, vec_part.at[3], spot.above(d))
+    for number in range(len(units) + 3, len(units) + DELAYS[-1]):
+        slot(number)
+    summed = vec_part[3]
+    for d in range(1, shards):
+        vec_copies[2 + d].wait_recv()
+        summed = summed + vec_land[2 + d]
+    r.sums[...] = summed
+    for copy in vec_copies:
+        copy.wait_send()
+    for kind, packs in zip(used, (r.mid_pack, r.proj_pack)):
+        for unit in kind[-packs.shape[0] :]:
+            unit.copies[0].wait_send()
+    for item in units + [w_kv, w_q, w_out, w_fc, w_proj]:
+        item.drain()
+    for item in (x_keys, x_values, x_query, x_d_out, x_stat):
+        item.drain()
+
+
+def whole_layer(**inputs):
+    shards, ctx_count = lax.axis_size("fsdp"), lax.axis_size("ctx")
+    rows, width = inputs.get("x").shape
+    hidden = inputs.get("fc_shard").shape[1]
+    low, wide = jnp.bfloat16, jnp.float32
+    dma = pltpu.SemaphoreType.DMA
+    chips, devices = ctx_count // 2, ctx_count * shards
+    mid = (width // devices, width)
+    tall = (hidden // devices, PROJ_COLS)
+    shapes = [mid] * (hidden // width) + [tall] * (width // PROJ_COLS) + [mid] * 4
+    vmem = pltpu.VMEM
+    scratch = dict(
+        qkv=vmem((width, 3 * width), low),
+        out=vmem((width, width), low),
+        fc=vmem((width, hidden), low),
+        proj=vmem((hidden, width), low),
+        kv=vmem((ctx_count, rows, 2 * width), low),
+        qd=vmem((ctx_count, rows, 2 * width), low),
+        stat=vmem((ctx_count, 4 * width // PAIR, rows), wide),
+        stat_mine=vmem((rows, 128), wide),
+        qpos=vmem((rows, 1), jnp.int32),
+        kpos=vmem((1, ctx_count * rows), jnp.int32),
+        first=vmem((rows, width), low),
+        attn=vmem((rows, width), wide),
+        attended=vmem((rows, width), low),
+        middle=vmem((rows, width), wide),
+        second=vmem((rows, width), low),
+        fc_line=vmem((1, hidden), wide),
+        act=vmem((rows, hidden), low),
+        d_pre=vmem((rows, hidden), low),
+        result=vmem((rows, width), wide),
+        d_second=vmem((rows, width), wide),
+        d_middle=vmem((rows, width), wide),
+        d_branch=vmem((rows, width), low),
+        d_qkv=vmem((rows, 3 * width), low),
+        vec_land=vmem((2 + shards, 16, width), wide),
+        vec_part=vmem((4, 16, width), wide),
+        mid_pack=vmem((3, chips, 2, shards) + mid, low),
+        proj_pack=vmem((2, chips, 2, shards) + tall, low),
+        own_sem=dma((4,)),
+        gather_send=dma((5, 5 * (shards - 1))),
+        gather_recv=dma((5, 5 * (shards - 1))),
+        ex_send=dma((5, 7)),
+        ex_recv=dma((5, 7)),
+        unit_send=dma((len(shapes), 3 + shards)),
+        unit_recv=dma((len(shapes), 3 + shards)),
+        vec_send=dma((2 + shards,)),
+        vec_recv=dma((2 + shards,)),
+    )
+    landings = []
+    for i, shape in enumerate(shapes):
+        if i in ALONG_FIRST:
+            landings += [
+                vmem((chips, shards) + shape, low),
+                vmem((2,) + shape, low),
+                vmem(shape, low),
+                vmem((shards - 1, chips) + shape, low),
+            ]
+            continue
+        landings += [
+            vmem((chips, shards) + shape, low),
+            vmem((2, shards) + shape, low),
+            vmem((shards,) + shape, low),
+            vmem((shards - 1,) + shape, low),
+        ]
+    outputs = dict(
+        layer_out=jax.ShapeDtypeStruct((rows, width), low),
+        grad_in=jax.ShapeDtypeStruct((rows, width), wide),
+        g_qkv=jax.ShapeDtypeStruct((width // devices, 3 * width), wide),
+        g_out=jax.ShapeDtypeStruct((width // devices, width), wide),
+        g_fc=jax.ShapeDtypeStruct((width // devices, hidden), wide),
+        g_proj=jax.ShapeDtypeStruct((hidden // devices, width), wide),
+        sums=jax.ShapeDtypeStruct((16, width), wide),
+    )
+    inside = pl.BlockSpec(memory_space=pltpu.VMEM)
+    anywhere = pl.BlockSpec(memory_space=pl.ANY)
+    return pl.pallas_call(
+        partial(layer_kernel, shards, (*inputs, *outputs, *scratch)),
+        in_specs=[pl.BlockSpec(memory_space=pltpu.SMEM)]
+        + [inside] * (len(inputs) - 5)
+        + [anywhere] * 4,
+        out_specs=[inside] * len(outputs),
+        out_shape=list(outputs.values()),
+        scratch_shapes=list(scratch.values()) + landings,
+        compiler_params=pltpu.CompilerParams(
+            collective_id=0, has_side_effects=True, vmem_limit_bytes=VMEM_LIMIT
+        ),
+        name="whole",
+    )(*inputs.values())
+
+
+VMEM_LIMIT = 62 * 2**20
+
+
+def finish_kernel(*refs):
+    ins, outs = refs[:7], refs[7:]
+    for src, dst in zip(ins[:6], outs[:6]):
+        dst[...] = src[...]
+    sums, small = ins[6], outs[6:]
+    shards = lax.axis_size("fsdp")
+    devices = lax.axis_size("ctx") * shards
+    device = lax.axis_index("ctx") * shards + lax.axis_index("fsdp")
+    width = sums.shape[1]
+
+    def piece(rows, start, size):
+        return pltpu.roll(rows, lax.rem(width - start, width), 1)[:, :size]
+
+    share = width // devices
+    lines = piece(sums[0:8], device * share, share)
+    for i in range(8):
+        small[i][...] = lines[i : i + 1]
+    share = small[8].shape[1]
+    fit = width // share
+    line = sums[pl.ds(8 + device // fit, 1), :]
+    eight = jnp.broadcast_to(line, (8, width))
+    small[8][...] = piece(eight, lax.rem(device, fit) * share, share)[0:1]
+
+
+def device_slices(*parts, shape):
+    devices = lax.axis_size("ctx") * lax.axis_size("fsdp")
+    width = parts[6].shape[1]
+    inside = pl.BlockSpec(memory_space=pltpu.VMEM)
+    shares = [width // devices] * 8 + [parts[4].shape[1] // devices]
+    outs = pl.pallas_call(
+        finish_kernel,
+        in_specs=[inside] * 7,
+        out_specs=[inside] * 15,
+        out_shape=[jax.ShapeDtypeStruct(p.shape, p.dtype) for p in parts[:6]]
+        + [jax.ShapeDtypeStruct((1, share), jnp.float32) for share in shares],
+        name="finish",
+    )(*parts)
+    layer_out, grad_in, g_qkv, g_out, g_fc, g_proj = outs[:6]
+    small = [item.reshape(-1) for item in outs[6:]]
+    return (
+        layer_out.reshape(shape),
+        grad_in.reshape(shape),
+        g_qkv,
+        small[0],
+        small[1],
+        g_out,
+        small[2],
+        g_fc,
+        small[8],
+        g_proj,
+        *small[3:8],
+    )
+
+
 def per_device(
     layer_in,
     qkv_weight,
@@ -524,6 +1354,26 @@
     ctx_count = lax.axis_size("ctx")
     shards = ctx_count * lax.axis_size("fsdp")
     _, _, rows, width = layer_in.shape
+    if ctx_count == 8:
+        outs = whole_layer(
+            table=pair_table,
+            x=layer_in.reshape(rows, width),
+            cot=cotangent.reshape(rows, width),
+            attn_gain=attn_norm_gain,
+            attn_shift=attn_norm_shift,
+            mlp_gain=mlp_norm_gain,
+            mlp_shift=mlp_norm_shift,
+            query_bias=query_bias,
+            value_bias=value_bias,
+            out_bias=out_bias,
+            proj_bias=proj_bias,
+            fc_bias=fc_bias,
+            qkv_shard=qkv_weight,
+            out_shard=out_weight,
+            fc_shard=fc_weight,
+            proj_shard=proj_weight,
+        )
+        return device_slices(*outs, shape=layer_in.shape)
     my_pos = block_positions(pair_table, lax.axis_index("ctx"), ctx_count)
     every_pos = all_positions(pair_table, ctx_count)
     flat_in = layer_in.reshape(rows, width).astype(jnp.float32)

time: 386 us -> 180 us (0.47)
  Pallas kernels: 231 us -> 179 us
  local copies, waits for them, and re-layouts: 47.4 us -> 0 us
  waiting for transfers between devices: 41.7 us -> 0 us
  matrix products: 29.2 us -> 0 us
  between operations: 15.8 us -> 0.84 us
  blocking collectives: 9.4 us -> 0 us
  other arithmetic: 8.63 us -> 0 us
    pallas_call x5 -> x2, Pallas kernels: 231 us -> 179 us  [the longest x1 176 us: whole_layer(): pl.pallas_call(partial(layer_kernel, shards, (*inputs, *outputs, *scratch...]
    all_gather x3 -> x0, waiting for transfers between devices: 41.7 us -> none  [the longest x1 41.7 us: per_device(): every_kv = lax.all_gather(keys_values, 'ctx', axis=0, tiled=True)]
    dot_general x13 -> x0, matrix products: 29.2 us -> none  [the longest x1 4.21 us: per_device(): jnp.einsum('tf,td->fd', act_low, d_result, preferred_element_type=jnp.flo...]
    unnamed x125 -> x0, local copies, waits for them, and re-layouts: 25 us -> none
    all_gather x1 -> x0, blocking collectives: 9.4 us -> none  [per_device(): lax.all_gather(jnp.transpose(stats, (0, 2, 1)).reshape(-1, rows), 'ctx',...]
    slice x8 -> x0, local copies, waits for them, and re-layouts: 7.64 us -> none  [the longest x2 2.85 us: per_device(): small.append(sum_small[start:start + size])]
    dynamic_slice x5 -> x0, local copies, waits for them, and re-layouts: 5.87 us -> none  [the longest x4 5.28 us: whole_weights(): lax.dynamic_slice_in_dim(item, lax.axis_index('ctx') * share, share, 0)]
    reduce_sum x7 -> x0, other arithmetic: 4.82 us -> none  [the longest x2 1.4 us: normalize(): jnp.mean(centered * centered, axis=-1, keepdims=True) + epsilon]
  transfers between devices with their start and end apart: 3 -> 0, of which waited for: 1 -> 0; matrix products, arithmetic and copies ran while one was open for 9% -> 0% of each run, Pallas kernels for 5% -> 0%
where the time goes in v3:
time: 180 us
  Pallas kernels  179 us (99%)
    pallas_call x1, Pallas kernels, whole_layer(): pl.pallas_call(partial(layer_kernel, shards, (*inputs, *outputs, *scratch...  176 us

profile of v3, /device:TPU:0, one launch (start us, length us, event | category | flops | bytes accessed | tf_op | source)
XLA Modules:
  0.0 180.0 jit_solution(1503994111777203852)
XLA Ops:
  0.7 176.4 %whole.1 = (bf16[192,768]{1,0:T(8,128)(2,1)}, f32[192,768]{1,0:T(8,128)}, f32[24,2304]{1,0:T(8,128)}, f32[24,768]{1,0:T(8,128)}, f32[24,3072]{1,0:T(8,128)}, /*index=5*/f32[96,768]{1,0:T(8,128)}, f32[16,768]{1,0:T(8,128)}) custom-call(s32[8]{0:T(128)} %refs_0_.1, bf16[192,768]{1,0:T(8,128)(2,1)} %bitcast.13, bf16[192,768]{1,0:T(8,128)(2,1)} %bitcast.14, ...), custom_call_target="tpu_custom_call" | custom-call | tf_op jit(solution)/shard_map/whole/pallas_call | solution.py:1264
  177.1 2.7 %finish.1 = (bf16[192,768]{1,0:T(8,128)(2,1)}, f32[192,768]{1,0:T(8,128)}, f32[24,2304]{1,0:T(8,128)}, f32[24,768]{1,0:T(8,128)}, f32[24,3072]{1,0:T(8,128)}, /*...) custom-call(bf16[192,768]{1,0:T(8,128)(2,1)} %get-tuple-element.37.r, ...), custom_call_target="tpu_custom_call" | custom-call | tf_op jit(solution)/shard_map/finish/pallas_call | solution.py:1311

commit v4 on v3

--- a/solution.py
+++ b/solution.py
@@ -789,8 +789,8 @@
 
 
 PROJ_COLS, TILE = 256, 256
-DELAYS = (0, 1, 3, 4, 5)
-DELAYS_ALONG = (0, 1, 5, 6, 7)
+DELAYS = (0, 1, 3, 5, 7)
+DELAYS_ALONG = (0, 1, 5, 7, 9)
 ALONG_FIRST = (0, 1)
 DIRECT = ()
 
@@ -814,6 +814,8 @@
             pltpu.make_async_copy(shard, whole.at[pl.ds(begin, size)], r.own_sem.at[i])
         )
         own[-1].start()
+    every_in = r.every_in
+    every_in[spot.me] = r.x[...]
     spot.greet()
 
     def gather(shard, whole, number, begin, columns):
@@ -821,11 +823,13 @@
         return Gather(spot, shard, whole, begin, columns, number in DIRECT, sems)
 
     hidden = r.fc.shape[1]
-    w_kv = gather(r.qkv_shard, r.qkv, 0, width, 2 * width)
-    w_q = gather(r.qkv_shard, r.qkv, 1, 0, width)
-    w_out = gather(r.out_shard, r.out, 2, 0, width)
-    w_fc = gather(r.fc_shard, r.fc, 3, 0, hidden)
-    w_proj = gather(r.proj_shard, r.proj, 4, 0, width)
+    w_k = gather(r.qkv_shard, r.qkv, 0, width, width)
+    w_v = gather(r.qkv_shard, r.qkv, 1, 2 * width, width)
+    w_q = gather(r.qkv_shard, r.qkv, 2, 0, width)
+    w_out = gather(r.out_shard, r.out, 3, 0, width)
+    w_fc = gather(r.fc_shard, r.fc, 4, 0, hidden)
+    w_proj = gather(r.proj_shard, r.proj, 5, 0, width)
+    gathers = (w_k, w_v, w_q, w_out, w_fc, w_proj)
 
     def exchange(number, view):
         return Exchange(spot, view, (r.ex_send.at[number], r.ex_recv.at[number]))
@@ -833,17 +837,16 @@
     def columns_of(ref, start):
         return lambda device: ref.at[device, :, pl.ds(start, width)]
 
-    x_keys = exchange(0, columns_of(kv, 0))
-    x_values = exchange(1, columns_of(kv, width))
-    x_query = exchange(2, columns_of(qd, 0))
-    x_d_out = exchange(3, columns_of(qd, width))
-    x_stat = exchange(4, lambda device: stat.at[device])
+    x_in = exchange(0, lambda device: r.every_in.at[device])
+    x_d_out = exchange(1, columns_of(qd, width))
+    x_stat = exchange(2, lambda device: stat.at[device])
 
     def vector(ref):
         return ref[...].reshape(1, -1)
 
-    w_kv.along()
-    w_q.along()
+    x_in.start()
+    for item in gathers:
+        item.along()
     table = r.table
 
     def spread(position, pair):
@@ -862,42 +865,54 @@
             (local >= 0) & (local < rows), spread(local, table[device]), key_pos
         )
     r.kpos[...] = key_pos
-    normed, _ = normalize(r.x[...].astype(jnp.float32))
-    r.first[...] = (normed * vector(r.attn_gain) + vector(r.attn_shift)).astype(low)
-    first_in = r.first[...]
-    w_kv.step_one()
-    w_out.along()
-    w_fc.along()
-    w_kv.step_two()
+    x_in.pass_on()
+    w_k.step_one()
+    w_v.step_one()
+    x_in.share()
+    w_k.step_two()
     w_q.step_one()
+    w_v.step_two()
+    x_in.finish()
+    x_in.drain()
+
+    @pl.loop(0, count)
+    def _(device):
+        normed, _ = normalize(every_in[device].astype(jnp.float32))
+        every_in[device] = (normed * vector(r.attn_gain) + vector(r.attn_shift)).astype(low)
+
+    def project(start, finish):
+        @pl.loop(0, count // 2)
+        def _(i):
+            two = pl.ds(2 * i, 2)
+            block = dot_nn(
+                every_in[two].reshape(2 * rows, width), r.qkv[:, pl.ds(start, width)]
+            )
+            finish(two, block)
+
+    def put_keys(two, block):
+        kv[two, :, pl.ds(0, width)] = block.astype(low).reshape(2, rows, width)
+
+    def put_values(two, block):
+        block = block + vector(r.value_bias)
+        kv[two, :, pl.ds(width, width)] = block.astype(low).reshape(2, rows, width)
+
+    def put_query(two, block):
+        block = (block + vector(r.query_bias)).astype(low) * jnp.bfloat16(HEAD_DIM ** (-0.5))
+        qd[two, :, pl.ds(0, width)] = block.reshape(2, rows, width)
+
+    w_out.step_one()
+    w_q.step_two()
     own[0].wait()
-    w_kv.complete()
-    kv[spot.me, :, pl.ds(0, width)] = dot_nn(
-        first_in, r.qkv[:, pl.ds(width, width)]
-    ).astype(low)
-    x_keys.start()
-    kv[spot.me, :, pl.ds(width, width)] = (
-        dot_nn(first_in, r.qkv[:, pl.ds(2 * width, width)]) + vector(r.value_bias)
-    ).astype(low)
-    x_values.start()
-    w_proj.along()
-    w_q.step_two()
-    x_keys.pass_on()
-    w_out.step_one()
-    x_values.pass_on()
+    w_k.complete()
+    project(width, put_keys)
+    w_fc.step_one()
+    w_v.complete()
+    w_out.step_two()
+    project(2 * width, put_values)
     w_q.complete()
-    qd[spot.me, :, pl.ds(0, width)] = (
-        (dot_nn(first_in, r.qkv[:, pl.ds(0, width)]) + vector(r.query_bias)).astype(low)
-        * jnp.bfloat16(HEAD_DIM ** (-0.5))
-    )
-    w_out.step_two()
-    w_fc.step_one()
-    x_keys.share()
-    x_values.share()
+    w_fc.step_two()
+    project(0, put_query)
     w_proj.step_one()
-    w_fc.step_two()
-    x_keys.finish()
-    x_values.finish()
 
     stat_lane = lax.broadcasted_iota(jnp.int32, r.stat_mine.shape, 1)
 
@@ -933,7 +948,8 @@
     w_out.complete()
     w_proj.step_two()
     pl.loop(2, 4)(attend)
-    x_query.start()
+    for d in range(1, shards):
+        w_fc.step_three(d)
     pl.loop(4, pairs)(attend)
     own[1].wait()
     attended = r.attn[...].astype(low)
@@ -943,7 +959,8 @@
     r.second[...] = (normed * vector(r.mlp_gain) + vector(r.mlp_shift)).astype(low)
     r.fc_line[...] = vector(r.fc_bias)
     own[2].wait()
-    w_fc.complete()
+    for d in range(1, shards):
+        w_fc.finish(d)
     own[3].wait()
     piece = hidden // shards
     for d in range(shards):
@@ -969,7 +986,6 @@
             r.d_second[...] = d_second
             for k in range(1, shards):
                 w_proj.step_three(k)
-            x_query.pass_on()
 
     units, makers = [], []
     used = ([], [])
@@ -1023,7 +1039,7 @@
         add(1, r.g_proj, n * PROJ_COLS, PROJ_COLS, lambda p, n=n: make_proj(p, n))
     add(0, r.g_out, 0, width, lambda p: make_rows(p, r.attended, r.d_branch, 0))
     for n in range(3):
-        add(0, r.g_qkv, n * width, width, lambda p, n=n: make_rows(p, r.first, r.d_qkv, n * width))
+        add(0, r.g_qkv, n * width, width, lambda p, n=n: make_rows(p, every_in.at[spot.me], r.d_qkv, n * width))
 
     def slot(number):
         if number < len(units):
@@ -1059,7 +1075,6 @@
     pl.loop(0, pairs)(deltas)
     stat[spot.me] = jnp.transpose(r.stat_mine[...])[: stat.shape[1]]
     x_stat.start()
-    x_query.share()
     slot(1)
     x_d_out.pass_on()
     x_stat.pass_on()
@@ -1109,24 +1124,25 @@
         r.d_qkv[:, lanes_of(h, 2 * width)] = head_pick(*value_parts).astype(low)
 
     slot(2)
+    slot(3)
     pl.loop(0, 2)(query_pair)
     x_d_out.share()
     x_stat.share()
-    slot(3)
+    slot(4)
     pl.loop(2, 4)(query_pair)
-    slot(4)
+    slot(5)
     pl.loop(4, pairs)(query_pair)
-    x_query.finish()
     x_d_out.finish()
     x_stat.finish()
-    slot(5)
+    slot(6)
     pl.loop(0, 2)(key_pair)
-    slot(6)
+    slot(7)
     pl.loop(2, 4)(key_pair)
-    slot(7)
+    slot(8)
     pl.loop(4, pairs)(key_pair)
-    for number in range(8, 11):
-        slot(number)
+    slot(9)
+    slot(10)
+    slot(11)
     d_qkv = r.d_qkv[...]
     d_first = dot_nt(d_qkv, r.qkv[...])
     normed, inverse = normalize(r.x[...].astype(jnp.float32))
@@ -1162,12 +1178,12 @@
 
     for k, other in enumerate((spot.sibling, spot.first, spot.second)):
         copy = vec_post(k, vec_part.at[k], spot.near(other))
-        slot(len(units) + k)
+        slot(len(units) + 1 + k)
         copy.wait_recv()
         vec_part[k + 1] = vec_part[k] + vec_land[k]
     for d in range(1, shards):
         vec_post(2 + d, vec_part.at[3], spot.above(d))
-    for number in range(len(units) + 3, len(units) + DELAYS[-1]):
+    for number in range(len(units) + 4, len(units) + DELAYS[-1]):
         slot(number)
     summed = vec_part[3]
     for d in range(1, shards):
@@ -1179,9 +1195,9 @@
     for kind, packs in zip(used, (r.mid_pack, r.proj_pack)):
         for unit in kind[-packs.shape[0] :]:
             unit.copies[0].wait_send()
-    for item in units + [w_kv, w_q, w_out, w_fc, w_proj]:
+    for item in (*units, *gathers):
         item.drain()
-    for item in (x_keys, x_values, x_query, x_d_out, x_stat):
+    for item in (x_d_out, x_stat):
         item.drain()
 
 
@@ -1207,7 +1223,7 @@
         stat_mine=vmem((rows, 128), wide),
         qpos=vmem((rows, 1), jnp.int32),
         kpos=vmem((1, ctx_count * rows), jnp.int32),
-        first=vmem((rows, width), low),
+        every_in=vmem((ctx_count, rows, width), low),
         attn=vmem((rows, width), wide),
         attended=vmem((rows, width), low),
         middle=vmem((rows, width), wide),
@@ -1225,10 +1241,10 @@
         mid_pack=vmem((3, chips, 2, shards) + mid, low),
         proj_pack=vmem((2, chips, 2, shards) + tall, low),
         own_sem=dma((4,)),
-        gather_send=dma((5, 5 * (shards - 1))),
-        gather_recv=dma((5, 5 * (shards - 1))),
-        ex_send=dma((5, 7)),
-        ex_recv=dma((5, 7)),
+        gather_send=dma((6, 5 * (shards - 1))),
+        gather_recv=dma((6, 5 * (shards - 1))),
+        ex_send=dma((3, 7)),
+        ex_recv=dma((3, 7)),
         unit_send=dma((len(shapes), 3 + shards)),
         unit_recv=dma((len(shapes), 3 + shards)),
         vec_send=dma((2 + shards,)),

time: 180 us -> 165 us (0.917)
  Pallas kernels: 179 us -> 164 us
    pallas_call x1, Pallas kernels: 176 us -> 161 us  [whole_layer(): pl.pallas_call(partial(layer_kernel, shards, (*inputs, *outputs, *scratch...]
where the time goes in v4:
time: 165 us; the launch traced here: 164 us
  Pallas kernels  164 us (99%)
    pallas_call x1, Pallas kernels, whole_layer(): pl.pallas_call(partial(layer_kernel, shards, (*inputs, *outputs, *scratch...  161 us

profile of v4, /device:TPU:0, one launch (start us, length us, event | category | flops | bytes accessed | tf_op | source)
XLA Modules:
  0.0 164.5 jit_solution(1604420502259256422)
XLA Ops:
  0.7 160.9 %whole.1 = (bf16[192,768]{1,0:T(8,128)(2,1)}, f32[192,768]{1,0:T(8,128)}, f32[24,2304]{1,0:T(8,128)}, f32[24,768]{1,0:T(8,128)}, f32[24,3072]{1,0:T(8,128)}, /*index=5*/f32[96,768]{1,0:T(8,128)}, f32[16,768]{1,0:T(8,128)}) custom-call(s32[8]{0:T(128)} %refs_0_.1, bf16[192,768]{1,0:T(8,128)(2,1)} %bitcast.13, bf16[192,768]{1,0:T(8,128)(2,1)} %bitcast.14, ...), custom_call_target="tpu_custom_call" | custom-call | tf_op jit(solution)/shard_map/whole/pallas_call | solution.py:1280
  161.6 2.7 %finish.1 = (bf16[192,768]{1,0:T(8,128)(2,1)}, f32[192,768]{1,0:T(8,128)}, f32[24,2304]{1,0:T(8,128)}, f32[24,768]{1,0:T(8,128)}, f32[24,3072]{1,0:T(8,128)}, /*...) custom-call(bf16[192,768]{1,0:T(8,128)(2,1)} %get-tuple-element.37.r, ...), custom_call_target="tpu_custom_call" | custom-call | tf_op jit(solution)/shard_map/finish/pallas_call | solution.py:1327

commit v5 on v4

--- a/solution.py
+++ b/solution.py
@@ -558,9 +558,8 @@
 
 
 class Gather:
-    def __init__(self, spot, shard, whole, begin, columns, direct, sems):
+    def __init__(self, spot, shard, whole, begin, columns, sems):
         self.spot, self.shard, self.whole, self.sems = spot, shard, whole, sems
-        self.direct = direct
         self.rows, self.begin, self.half = shard.shape[0], begin, columns // 2
         self.copies = {}
 
@@ -580,27 +579,24 @@
     def along(self):
         spot, quarter = self.spot, self.rows // 4
         start = (2 * spot.b + spot.a) * quarter
-        if self.direct:
-            quarter, start = self.rows, 0
         src = self.shard.at[pl.ds(pl.multiple_of(start, 16), quarter), self.cols()]
         for d in range(1, spot.shards):
             self.post(0, d, src, self.part(spot.row, start, quarter), spot.above(d))
 
-    def step_one(self):
+    def steps(self, d):
+        return (d,) if d else range(1, self.spot.shards)
+
+    def step_one(self, only=None):
         spot, quarter = self.spot, self.rows // 4
-        if self.direct:
-            return
         start = (2 * spot.b + spot.a) * quarter
-        for d in range(1, spot.shards):
+        for d in self.steps(only):
             self.copies[0, d].wait_recv()
             ref = self.part(spot.came(d), start, quarter)
             self.post(1, d, ref, ref, spot.near(spot.first))
 
-    def step_two(self):
+    def step_two(self, only=None):
         spot, half = self.spot, self.rows // 2
-        if self.direct:
-            return
-        for d in range(1, spot.shards):
+        for d in self.steps(only):
             self.copies[1, d].wait_recv()
             ref = self.part(spot.came(d), spot.b * half, half)
             self.post(2, d, ref, ref, spot.near(spot.second))
@@ -608,18 +604,12 @@
 
     def step_three(self, d):
         spot, half = self.spot, self.rows // 2
-        if self.direct:
-            self.copies[0, d].wait_recv()
-            ref = self.part(spot.came(d), 0, self.rows)
-            self.post(4, d, ref, ref, spot.near(spot.sibling))
-            return
         self.copies[2, d].wait_recv()
         ref = self.part(spot.came(d), (1 - spot.b) * half, half)
         self.post(4, d, ref, ref, spot.near(spot.sibling))
 
     def finish(self, d):
-        if not self.direct:
-            self.copies[3, d].wait_recv()
+        self.copies[3, d].wait_recv()
         self.copies[4, d].wait_recv()
 
     def complete(self):
@@ -790,9 +780,8 @@
 
 PROJ_COLS, TILE = 256, 256
 DELAYS = (0, 1, 3, 5, 7)
-DELAYS_ALONG = (0, 1, 5, 7, 9)
+DELAYS_ALONG = (0, 1, 7, 9, 10)
 ALONG_FIRST = (0, 1)
-DIRECT = ()
 
 
 def layer_kernel(shards, names, *refs):
@@ -820,7 +809,7 @@
 
     def gather(shard, whole, number, begin, columns):
         sems = r.gather_send.at[number], r.gather_recv.at[number]
-        return Gather(spot, shard, whole, begin, columns, number in DIRECT, sems)
+        return Gather(spot, shard, whole, begin, columns, sems)
 
     hidden = r.fc.shape[1]
     w_k = gather(r.qkv_shard, r.qkv, 0, width, width)
@@ -1041,13 +1030,15 @@
     for n in range(3):
         add(0, r.g_qkv, n * width, width, lambda p, n=n: make_rows(p, every_in.at[spot.me], r.d_qkv, n * width))
 
+    starts = [*range(9), 10, 11]
+
     def slot(number):
-        if number < len(units):
-            makers[number]()
+        if number in starts:
+            makers[starts.index(number)]()
         for stage in range(1, 5):
             for i, unit in enumerate(units):
                 delays = DELAYS_ALONG if i in ALONG_FIRST else DELAYS
-                if number - i == delays[stage]:
+                if number - starts[i] == delays[stage]:
                     (unit.step_one, unit.step_two, unit.along, unit.finish)[stage - 1]()
 
     slot(0)
@@ -1125,24 +1116,25 @@
 
     slot(2)
     slot(3)
-    pl.loop(0, 2)(query_pair)
+    slot(4)
     x_d_out.share()
     x_stat.share()
-    slot(4)
+    pl.loop(0, 2)(query_pair)
+    slot(5)
     pl.loop(2, 4)(query_pair)
-    slot(5)
+    slot(6)
     pl.loop(4, pairs)(query_pair)
     x_d_out.finish()
     x_stat.finish()
-    slot(6)
+    slot(7)
     pl.loop(0, 2)(key_pair)
-    slot(7)
+    slot(8)
     pl.loop(2, 4)(key_pair)
-    slot(8)
+    slot(9)
     pl.loop(4, pairs)(key_pair)
-    slot(9)
     slot(10)
     slot(11)
+    slot(12)
     d_qkv = r.d_qkv[...]
     d_first = dot_nt(d_qkv, r.qkv[...])
     normed, inverse = normalize(r.x[...].astype(jnp.float32))
@@ -1178,12 +1170,12 @@
 
     for k, other in enumerate((spot.sibling, spot.first, spot.second)):
         copy = vec_post(k, vec_part.at[k], spot.near(other))
-        slot(len(units) + 1 + k)
+        slot(13 + k)
         copy.wait_recv()
         vec_part[k + 1] = vec_part[k] + vec_land[k]
     for d in range(1, shards):
         vec_post(2 + d, vec_part.at[3], spot.above(d))
-    for number in range(len(units) + 4, len(units) + DELAYS[-1]):
+    for number in range(16, 12 + DELAYS[-1]):
         slot(number)
     summed = vec_part[3]
     for d in range(1, shards):

time: 165 us -> 162 us (0.982)
  Pallas kernels: 164 us -> 161 us
    pallas_call x1, Pallas kernels: 161 us -> 159 us  [whole_layer(): pl.pallas_call(partial(layer_kernel, shards, (*inputs, *outputs, *scratch...]
where the time goes in v5:
time: 162 us
  Pallas kernels  161 us (99%)
    pallas_call x1, Pallas kernels, whole_layer(): pl.pallas_call(partial(layer_kernel, shards, (*inputs, *outputs, *scratch...  159 us

profile of v5, /device:TPU:0, one launch (start us, length us, event | category | flops | bytes accessed | tf_op | source)
XLA Modules:
  0.0 162.2 jit_solution(5567302592588845694)
XLA Ops:
  0.7 158.7 %whole.1 = (bf16[192,768]{1,0:T(8,128)(2,1)}, f32[192,768]{1,0:T(8,128)}, f32[24,2304]{1,0:T(8,128)}, f32[24,768]{1,0:T(8,128)}, f32[24,3072]{1,0:T(8,128)}, /*index=5*/f32[96,768]{1,0:T(8,128)}, f32[16,768]{1,0:T(8,128)}) custom-call(s32[8]{0:T(128)} %refs_0_.1, bf16[192,768]{1,0:T(8,128)(2,1)} %bitcast.13, bf16[192,768]{1,0:T(8,128)(2,1)} %bitcast.14, ...), custom_call_target="tpu_custom_call" | custom-call | tf_op jit(solution)/shard_map/whole/pallas_call | solution.py:1272
  159.3 2.7 %finish.1 = (bf16[192,768]{1,0:T(8,128)(2,1)}, f32[192,768]{1,0:T(8,128)}, f32[24,2304]{1,0:T(8,128)}, f32[24,768]{1,0:T(8,128)}, f32[24,3072]{1,0:T(8,128)}, /*...) custom-call(bf16[192,768]{1,0:T(8,128)(2,1)} %get-tuple-element.37.r, ...), custom_call_target="tpu_custom_call" | custom-call | tf_op jit(solution)/shard_map/finish/pallas_call | solution.py:1319
